TPU v7x, 128 devices: a whole 4x4x4 slice. The times are simulated.
128 devices in a mesh: dp: 8 (over y, core), ctx: 16 (over z, x).
Axes of the slice: x: 4, y: 4, z: 4, core: 2. Of those that a mesh axis runs over, the one named last changes fastest.
Arguments:
- block_in: bfloat16 [16, 2048, 1024], P('dp', 'ctx'), may hold values from -6 to 6
- segment_ids: int32 [16, 2048], P('dp'), may hold values from -1 to 34, as said below
- attn_gain: float32 [1024], replicated, may hold values from 0.1 to 1.9
- w_query: bfloat16 [1024, 1024], P(('dp', 'ctx')), may hold values from -0.1875 to 0.1875
- w_key: bfloat16 [1024, 512], P(('dp', 'ctx')), may hold values from -0.1875 to 0.1875
- w_value: bfloat16 [1024, 512], P(('dp', 'ctx')), may hold values from -0.1875 to 0.1875
- query_gain: float32 [64], replicated, may hold values from 0.1 to 1.9
- key_gain: float32 [64], replicated, may hold values from 0.1 to 1.9
- w_out: bfloat16 [1024, 1024], P(('dp', 'ctx')), may hold values from -2 to 2
- ffn_gain: float32 [1024], replicated, may hold values from 0.1 to 1.9
- w_gate: bfloat16 [1024, 4608], P(('dp', 'ctx')), may hold values from -0.1875 to 0.1875
- w_up: bfloat16 [1024, 4608], P(('dp', 'ctx')), may hold values from -0.1875 to 0.1875
- w_down: bfloat16 [4608, 1024], P(('dp', 'ctx')), may hold values from -0.09375 to 0.09375
- out_grad: bfloat16 [16, 2048, 1024], P('dp', 'ctx'), may hold values from -6 to 6
Outputs:
- block_out: bfloat16 [16, 2048, 1024], P('dp', 'ctx')
- block_in_grad: bfloat16 [16, 2048, 1024], P('dp', 'ctx')
- grad_query: float32 [1024, 1024], P(('dp', 'ctx'))
- grad_key: float32 [1024, 512], P(('dp', 'ctx'))
- grad_value: float32 [1024, 512], P(('dp', 'ctx'))
- grad_out: float32 [1024, 1024], P(('dp', 'ctx'))
- grad_gate: float32 [1024, 4608], P(('dp', 'ctx'))
- grad_up: float32 [1024, 4608], P(('dp', 'ctx'))
- grad_down: float32 [4608, 1024], P(('dp', 'ctx'))
- grad_attn_gain: float32 [1024], replicated
- grad_query_gain: float32 [64], replicated
- grad_key_gain: float32 [64], replicated
- grad_ffn_gain: float32 [1024], replicated
Inputs may be any that keep to these rules, and one draw needn't show every extreme that they name: `segment_ids`: each sequence ends in 1 to 64 padding tokens of id -1. In each group of 2 sequences of one index of dp, one sequence holds a first document numbered 0 of fewer than 128 tokens and a second one numbered 2048 // 60 up to the padding; the others hold documents of 60 to 800 tokens numbered 0, 1, 2 and so on, the last one cut short by the padding.
All inputs are finite; a program needn't handle non-finite values.
Results may differ from a plain program's by a relative error of at most 0.018.
Values may be sent and summed in bfloat16 or wider, within the bound.
A program may use at most 256 MiB of HBM per device.

v0:
```python
import jax
import jax.numpy as jnp
from jax import lax
from jax.sharding import PartitionSpec as P

H = 16
KVH = 8
HDIM = 64


EPSILON = 1e-05
THETA_BASE = 1000000.0


def norm_forward(inputs, gain_vec):
    factor = lax.rsqrt(jnp.mean(inputs * inputs, axis=-1, keepdims=True) + EPSILON)
    normed = inputs * factor
    return (normed * gain_vec, normed, factor)


def norm_backward(upstream, gain_vec, normed, factor):
    scaled = upstream * gain_vec
    result = factor * (scaled - normed * jnp.mean(scaled * normed, axis=-1, keepdims=True))
    return (result, upstream * normed)


def rope_tables(places, head_dim):
    frequency = THETA_BASE ** (-jnp.arange(0, head_dim, 2, dtype=jnp.float32) / head_dim)
    angles = places.astype(jnp.float32)[:, None] * frequency[None, :]
    cosine = jnp.concatenate([jnp.cos(angles), jnp.cos(angles)], axis=-1)
    sine_rows = jnp.concatenate([jnp.sin(angles), jnp.sin(angles)], axis=-1)
    return (cosine, sine_rows)


def rotate(inputs, cosine, sine_rows):
    half_dim = inputs.shape[-1] // 2
    turned = jnp.concatenate([-inputs[..., half_dim:], inputs[..., :half_dim]], axis=-1)
    return inputs * cosine + turned * sine_rows


def across_rows(left, right):
    return lax.dot_general(
        left, right, (((0,), (0,)), ((), ())), preferred_element_type=jnp.float32
    )


def against_cols(left, right):
    return lax.dot_general(
        left, right, (((1,), (1,)), ((), ())), preferred_element_type=jnp.float32
    )


def local(
    block_in,
    segment_ids,
    attn_gain,
    w_query,
    w_key,
    w_value,
    query_gain,
    key_gain,
    w_out,
    ffn_gain,
    w_gate,
    w_up,
    w_down,
    out_grad,
):
    seq_count, span_len, model_width = block_in.shape
    seq_len = segment_ids.shape[1]
    head_count = H
    kv_count = KVH
    head_dim = HDIM
    group_size = head_count // kv_count
    kv_width = kv_count * head_dim
    all_width = head_count * head_dim
    row_count = seq_count * span_len
    score_scale = head_dim ** (-0.5)
    first_row = lax.axis_index("ctx") * span_len
    query_places = first_row + jnp.arange(span_len, dtype=jnp.int32)
    key_places = jnp.arange(seq_len, dtype=jnp.int32)
    query_segments = lax.dynamic_slice_in_dim(segment_ids, first_row, span_len, 1)
    cosine, sine_rows = rope_tables(query_places, head_dim)
    cosine = jnp.tile(cosine, (seq_count, 1))[:, None, :]
    sine_rows = jnp.tile(sine_rows, (seq_count, 1))[:, None, :]
    inputs = block_in.astype(jnp.float32).reshape(row_count, model_width)
    query_mat, key_mat, value_mat, out_mat = (
        lax.all_gather(w_query, ("dp", "ctx"), axis=0, tiled=True),
        lax.all_gather(w_key, ("dp", "ctx"), axis=0, tiled=True),
        lax.all_gather(w_value, ("dp", "ctx"), axis=0, tiled=True),
        lax.all_gather(w_out, ("dp", "ctx"), axis=0, tiled=True),
    )
    normed_in, unit_in, factor_in = norm_forward(inputs, attn_gain)
    low_in = normed_in.astype(jnp.bfloat16)
    query_raw = jnp.dot(low_in, query_mat, preferred_element_type=jnp.float32).reshape(
        row_count, head_count, head_dim
    )
    key_raw = jnp.dot(low_in, key_mat, preferred_element_type=jnp.float32).reshape(
        row_count, kv_count, head_dim
    )
    value_low = jnp.dot(low_in, value_mat, preferred_element_type=jnp.float32).astype(jnp.bfloat16)
    query_normed, query_unit, query_factor = norm_forward(query_raw, query_gain)
    query_low = rotate(query_normed, cosine, sine_rows).astype(jnp.bfloat16)
    key_normed, key_unit, key_factor = norm_forward(key_raw, key_gain)
    key_low = rotate(key_normed, cosine, sine_rows).astype(jnp.bfloat16)
    key_local = key_low.reshape(seq_count, span_len, kv_width)
    value_local = value_low.reshape(seq_count, span_len, kv_width)
    key_seq, value_seq = (
        lax.all_gather(key_local, "ctx", axis=1, tiled=True),
        lax.all_gather(value_local, "ctx", axis=1, tiled=True),
    )
    query_items = query_low.reshape(seq_count, span_len, kv_count, group_size, head_dim)

    def masked_scores(query_block, key_block, seg_row, seg_query):
        key_heads = key_block.reshape(seq_len, kv_count, head_dim)
        scores = (
            jnp.einsum("qkgd,tkd->kgqt", query_block, key_heads, preferred_element_type=jnp.float32)
            * score_scale
        )
        allowed = (seg_query[:, None] == seg_row[None, :]) & (
            query_places[:, None] >= key_places[None, :]
        )
        return jnp.where(allowed, scores, -1e30)

    def attend(entries):
        query_block, key_block, value_block, seg_row, seg_query = entries
        scores = masked_scores(query_block, key_block, seg_row, seg_query)
        top_score = jnp.max(scores, axis=-1, keepdims=True)
        exponent = jnp.exp(scores - top_score)
        totals = jnp.sum(exponent, axis=-1, keepdims=True)
        weights = exponent / totals
        value_heads = value_block.reshape(seq_len, kv_count, head_dim)
        mixed_out = jnp.einsum(
            "kgqt,tkd->qkgd",
            weights.astype(jnp.bfloat16),
            value_heads,
            preferred_element_type=jnp.float32,
        )
        return (
            mixed_out.reshape(span_len, all_width).astype(jnp.bfloat16),
            top_score + jnp.log(totals),
        )

    attended, log_totals = lax.map(
        attend, (query_items, key_seq, value_seq, segment_ids, query_segments)
    )
    attended = attended.reshape(row_count, all_width)
    residual = inputs + jnp.dot(attended, out_mat, preferred_element_type=jnp.float32)
    gate_mat, up_mat, down_mat = (
        lax.all_gather(w_gate, ("dp", "ctx"), axis=0, tiled=True),
        lax.all_gather(w_up, ("dp", "ctx"), axis=0, tiled=True),
        lax.all_gather(w_down, ("dp", "ctx"), axis=0, tiled=True),
    )
    normed_mid, unit_mid, factor_mid = norm_forward(residual, ffn_gain)
    low_mid = normed_mid.astype(jnp.bfloat16)
    gate_val = jnp.dot(low_mid, gate_mat, preferred_element_type=jnp.float32)
    up_val = jnp.dot(low_mid, up_mat, preferred_element_type=jnp.float32)
    gate_sig = jax.nn.sigmoid(gate_val)
    silu_val = gate_val * gate_sig
    hidden = (silu_val * up_val).astype(jnp.bfloat16)
    output = residual + jnp.dot(hidden, down_mat, preferred_element_type=jnp.float32)
    block_out = output.astype(jnp.bfloat16).reshape(seq_count, span_len, model_width)
    gate_mat, up_mat, down_mat = (
        lax.all_gather(w_gate, ("dp", "ctx"), axis=0, tiled=True),
        lax.all_gather(w_up, ("dp", "ctx"), axis=0, tiled=True),
        lax.all_gather(w_down, ("dp", "ctx"), axis=0, tiled=True),
    )
    query_mat, key_mat, value_mat, out_mat = (
        lax.all_gather(w_query, ("dp", "ctx"), axis=0, tiled=True),
        lax.all_gather(w_key, ("dp", "ctx"), axis=0, tiled=True),
        lax.all_gather(w_value, ("dp", "ctx"), axis=0, tiled=True),
        lax.all_gather(w_out, ("dp", "ctx"), axis=0, tiled=True),
    )
    key_seq, value_seq = (
        lax.all_gather(key_local, "ctx", axis=1, tiled=True),
        lax.all_gather(value_local, "ctx", axis=1, tiled=True),
    )
    down_low = out_grad.reshape(row_count, model_width)
    grad_down = across_rows(hidden, down_low)
    hidden_grad = against_cols(down_low, down_mat)
    slope = gate_sig * (1.0 + gate_val * (1.0 - gate_sig))
    gate_grad = (hidden_grad * up_val * slope).astype(jnp.bfloat16)
    up_grad = (hidden_grad * silu_val).astype(jnp.bfloat16)
    grad_gate = across_rows(low_mid, gate_grad)
    grad_up = across_rows(low_mid, up_grad)
    mlp_shards = (
        lax.psum_scatter(grad_gate, ("dp", "ctx"), scatter_dimension=0, tiled=True),
        lax.psum_scatter(grad_up, ("dp", "ctx"), scatter_dimension=0, tiled=True),
        lax.psum_scatter(grad_down, ("dp", "ctx"), scatter_dimension=0, tiled=True),
    )
    mid_grad = against_cols(gate_grad, gate_mat) + against_cols(up_grad, up_mat)
    resid_part, ffn_terms = norm_backward(mid_grad, ffn_gain, unit_mid, factor_mid)
    resid_grad = out_grad.astype(jnp.float32).reshape(row_count, model_width) + resid_part
    branch_low = resid_grad.astype(jnp.bfloat16)
    grad_out = across_rows(attended, branch_low)
    attended_grad = against_cols(branch_low, out_mat).astype(jnp.bfloat16)

    def attend_back(entries):
        query_block, key_block, value_block, seg_row, seg_query, log_block, upstream = entries
        scores = masked_scores(query_block, key_block, seg_row, seg_query)
        weights = jnp.exp(scores - log_block)
        weights_low = weights.astype(jnp.bfloat16)
        key_heads = key_block.reshape(seq_len, kv_count, head_dim)
        value_heads = value_block.reshape(seq_len, kv_count, head_dim)
        upstream_heads = upstream.reshape(span_len, kv_count, group_size, head_dim)
        weight_grad = jnp.einsum(
            "qkgd,tkd->kgqt", upstream_heads, value_heads, preferred_element_type=jnp.float32
        )
        value_terms = jnp.einsum(
            "kgqt,qkgd->tkd", weights_low, upstream_heads, preferred_element_type=jnp.float32
        )
        row_dots = jnp.sum(weights * weight_grad, axis=-1, keepdims=True)
        score_grad = (weights * (weight_grad - row_dots)).astype(jnp.bfloat16)
        query_terms = (
            jnp.einsum("kgqt,tkd->qkgd", score_grad, key_heads, preferred_element_type=jnp.float32)
            * score_scale
        )
        key_terms = (
            jnp.einsum(
                "kgqt,qkgd->tkd", score_grad, query_block, preferred_element_type=jnp.float32
            )
            * score_scale
        )
        return (
            query_terms.reshape(span_len, all_width),
            key_terms.reshape(seq_len, kv_width),
            value_terms.reshape(seq_len, kv_width),
        )

    query_rot_grad, key_seq_terms, value_seq_terms = lax.map(
        attend_back,
        (
            query_items,
            key_seq,
            value_seq,
            segment_ids,
            query_segments,
            log_totals,
            attended_grad.reshape(seq_count, span_len, all_width),
        ),
    )
    key_sums, value_sums = (
        lax.psum_scatter(
            key_seq_terms.astype(jnp.bfloat16), "ctx", scatter_dimension=1, tiled=True
        ).astype(jnp.float32),
        lax.psum_scatter(
            value_seq_terms.astype(jnp.bfloat16), "ctx", scatter_dimension=1, tiled=True
        ).astype(jnp.float32),
    )
    query_back = (
        lax.optimization_barrier(query_rot_grad.astype(jnp.bfloat16))
        .astype(jnp.float32)
        .reshape(row_count, head_count, head_dim)
    )
    key_back = (
        lax.optimization_barrier(key_sums.astype(jnp.bfloat16))
        .astype(jnp.float32)
        .reshape(row_count, kv_count, head_dim)
    )
    value_grad = value_sums.astype(jnp.bfloat16).reshape(row_count, kv_width)
    query_pre, query_gain_terms = norm_backward(
        rotate(query_back, cosine, -sine_rows), query_gain, query_unit, query_factor
    )
    key_pre, key_gain_terms = norm_backward(
        rotate(key_back, cosine, -sine_rows), key_gain, key_unit, key_factor
    )
    query_grad = query_pre.reshape(row_count, all_width).astype(jnp.bfloat16)
    key_grad = key_pre.reshape(row_count, kv_width).astype(jnp.bfloat16)
    grad_query = across_rows(low_in, query_grad)
    grad_key = across_rows(low_in, key_grad)
    grad_value = across_rows(low_in, value_grad)
    attn_shards = (
        lax.psum_scatter(grad_query, ("dp", "ctx"), scatter_dimension=0, tiled=True),
        lax.psum_scatter(grad_key, ("dp", "ctx"), scatter_dimension=0, tiled=True),
        lax.psum_scatter(grad_value, ("dp", "ctx"), scatter_dimension=0, tiled=True),
        lax.psum_scatter(grad_out, ("dp", "ctx"), scatter_dimension=0, tiled=True),
    )
    in_grad = (
        against_cols(query_grad, query_mat)
        + against_cols(key_grad, key_mat)
        + against_cols(value_grad, value_mat)
    )
    input_part, attn_terms = norm_backward(in_grad, attn_gain, unit_in, factor_in)
    block_in_grad = (
        (resid_grad + input_part).astype(jnp.bfloat16).reshape(seq_count, span_len, model_width)
    )
    gain_sums = lax.psum(
        (
            jnp.sum(attn_terms, axis=0),
            jnp.sum(query_gain_terms, axis=(0, 1)),
            jnp.sum(key_gain_terms, axis=(0, 1)),
            jnp.sum(ffn_terms, axis=0),
        ),
        ("dp", "ctx"),
    )
    return (
        block_out,
        block_in_grad,
        attn_shards[0],
        attn_shards[1],
        attn_shards[2],
        attn_shards[3],
        mlp_shards[0],
        mlp_shards[1],
        mlp_shards[2],
        gain_sums[0],
        gain_sums[1],
        gain_sums[2],
        gain_sums[3],
    )


def solution(mesh):
    return jax.shard_map(
        local,
        mesh=mesh,
        in_specs=(
            P("dp", "ctx", None),
            P("dp", None),
            P(),
            P(("dp", "ctx"), None),
            P(("dp", "ctx"), None),
            P(("dp", "ctx"), None),
            P(),
            P(),
            P(("dp", "ctx"), None),
            P(),
            P(("dp", "ctx"), None),
            P(("dp", "ctx"), None),
            P(("dp", "ctx"), None),
            P("dp", "ctx", None),
        ),
        out_specs=(
            P("dp", "ctx", None),
            P("dp", "ctx", None),
            P(("dp", "ctx"), None),
            P(("dp", "ctx"), None),
            P(("dp", "ctx"), None),
            P(("dp", "ctx"), None),
            P(("dp", "ctx"), None),
            P(("dp", "ctx"), None),
            P(("dp", "ctx"), None),
            P(),
            P(),
            P(),
            P(),
        ),
        check_vma=False,
    )
```

profile of v0, /device:TPU:0, one launch (start us, length us, event | category | flops | bytes accessed | tf_op | source)
XLA Modules:
  0.0 3998.0 jit_solution(14311289064054321407)
XLA Ops:
  12.0 64.9 %all-gather.11.cloned.1.call-done = bf16[1024,512]{1,0:T(8,128)(2,1)} async-done(((bf16[8,512]{1,0:T(8,128)(2,1)}), bf16[1024,512]{1,0:T(8,128)(2,1)}) %all-gather.11.cloned.1.call-update) | async-done | bytes 1048592 | tf_op jit(solution)/shard_map/all_gather | solution.py:90
  80.6 60.1 %all-gather.15.cloned.1.call-done = bf16[1024,512]{1,0:T(8,128)(2,1)} async-done(((bf16[8,512]{1,0:T(8,128)(2,1)}), bf16[1024,512]{1,0:T(8,128)(2,1)}) %all-gather.15.cloned.1.call-update) | async-done | bytes 1048592 | tf_op jit(solution)/shard_map/all_gather | solution.py:89
  148.4 58.0 %all-gather.19.cloned.1.call-done = bf16[1024,1024]{1,0:T(8,128)(2,1)} async-done(((bf16[8,1024]{1,0:T(8,128)(2,1)}), bf16[1024,1024]{1,0:T(8,128)(2,1)}) %all-gather.19.cloned.1.call-update) | async-done | bytes 2097168 | tf_op jit(solution)/shard_map/all_gather | solution.py:88
  211.7 51.9 %all-gather.13.cloned.1.call-done = bf16[2,2048,512]{1,2,0:T(8,128)(2,1)} async-done(((bf16[2,128,512]{1,2,0:T(8,128)(2,1)}), bf16[2,2048,512]{1,2,0:T(8,128)(2,1)}) %all-gather.13.cloned.1.call-update) | async-done | bytes 4194320 | tf_op jit(solution)/shard_map/all_gather | solution.py:110
  263.6 59.0 %all-gather.17.cloned.1.call-done = bf16[2,2048,512]{1,2,0:T(8,128)(2,1)} async-done(((bf16[2,128,512]{1,2,0:T(8,128)(2,1)}), bf16[2,2048,512]{1,2,0:T(8,128)(2,1)}) %all-gather.17.cloned.1.call-update) | async-done | bytes 4194320 | tf_op jit(solution)/shard_map/all_gather | solution.py:109
  322.6 57.0 %while.28 = (s32[]{:T(128)}, bf16[2,128,1024]{2,1,0:T(8,128)(2,1)S(1)}, f32[2,8,2,128,1]{3,2,1,4,0:T(2,128)S(1)}, bf16[2,2048,512]{1,2,0:T(8,128)(2,1)}, s32[2,1...) while((s32[]{:T(128)}, ...), condition=%wide.region_6.7_spmd.clone, body=%wide.region_3.6_spmd.clone.sunk | while | flops 1124989056 | bytes 65628808 | solution.py:144
  333.6 9.2 fusion.142
  379.6 10.3 all-gather.21.cloned.1.call-done
  392.7 69.4 %all-gather.27.cloned.1.call-done = bf16[128,36,1024]{2,1,0:T(8,128)(2,1)} async-done(((bf16[1,36,1024]{2,1,0:T(8,128)(2,1)}), bf16[128,36,1024]{2,1,0:T(8,128)(2,1)}) %all-gather.27.cloned.1.call-update) | async-done | bytes 9437200 | tf_op jit(solution)/shard_map/all_gather | solution.py:152
  462.1 13.1 reshape.319
  475.2 58.7 %all-gather.25.cloned.1.call-done = bf16[1024,4608]{1,0:T(8,128)(2,1)} async-done(((bf16[8,4608]{1,0:T(8,128)(2,1)}), bf16[1024,4608]{1,0:T(8,128)(2,1)}) %all-gather.25.cloned.1.call-update) | async-done | bytes 9437200 | tf_op jit(solution)/shard_map/all_gather | solution.py:151
  542.4 62.8 %all-gather.23.cloned.1.call-done = bf16[1024,4608]{1,0:T(8,128)(2,1)} async-done(((bf16[8,4608]{1,0:T(8,128)(2,1)}), bf16[1024,4608]{1,0:T(8,128)(2,1)}) %all-gather.23.cloned.1.call-update) | async-done | bytes 9437200 | tf_op jit(solution)/shard_map/all_gather | solution.py:150
  637.2 138.6 %while.29 = (s32[]{:T(128)}, bf16[2,128,1024]{1,2,0:T(8,128)(2,1)}, bf16[2,2048,512]{1,2,0:T(8,128)(2,1)}, bf16[2,2048,512]{2,1,0:T(8,128)(2,1)}, bf16[2,2048,51...) while((s32[]{:T(128)}, bf16[2,128,1024]{1,2,0:T(8,128)(2,1)}, ...), condition=%wide.region_11.12_spmd.clone, body=%wide.region_9.11_spmd.clone.sunk | while | flops 2750412800 | bytes 304041024 | solution.py:230
  652.9 11.0 fusion.159
  668.3 15.8 fusion.157
  722.1 11.0 fusion.159
  737.4 15.9 fusion.157
  776.0 11.2 copy.85
  801.0 50.4 %reduce-scatter.13.cloned.1.call-done = bf16[2,128,512]{2,1,0:T(8,128)(2,1)} async-done(((bf16[2,2048,512]{2,1,0:T(8,128)(2,1)}), bf16[2,128,512]{2,1,0:T(8,128)(2,1)}) %reduce-scatter.13.cloned.1.call-update) | async-done | bytes 262160 | tf_op jit(solution)/shard_map/reduce_scatter | solution.py:246
  854.2 77.8 %reduce-scatter.27.cloned.1.call-done = bf16[128,1024]{1,0:T(8,128)(2,1)} async-done(((bf16[2048,1024]{1,0:T(8,128)(2,1)}), bf16[128,1024]{1,0:T(8,128)(2,1)}) %reduce-scatter.27.cloned.1.call-update) | async-done | bytes 262160
  940.0 9.5 fusion.63
  949.6 9.6 fusion.62
  960.2 9.5 fusion.64
  969.7 400.3 %fusion.8 = f32[40,1024]{1,0:T(8,128)} fusion(f32[4608,1024]{1,0:T(8,128)} %fusion.64), kind=kCustom, calls=%all-reduce-scatter | all-reduce-scatter fusion | flops 5242881 | bytes 19038208
  1418.6 21.9 concatenate.24
  1445.9 73.8 %all-reduce.2 = (f32[1024]{0:T(1024)}, f32[64]{0:T(128)}, f32[64]{0:T(128)}, f32[1024]{0:T(1024)}) all-reduce(f32[1024]{0:T(1024)S(1)} %get-tuple-element.257, f32[64]{0:T(128)S(1)} %get-tuple-element.253, f32[64]{0:T(128)S(1)} %copy-done.68, f32[1024]{0:T(1024)S(1)} %copy-done.67), channel_id=1, replica_groups=mesh['dp'=8,'ctx'=16] {'dp','ctx'}, use_global_device_ids=true, to_apply=%region_25.26 | all-reduce | flops 2176 | bytes 17408 | tf_op jit(solution)/shard_map/psum | solution.py:287
  1522.0 74.4 %reduce-scatter.15.cloned.1.call-done = f32[8,1024]{1,0:T(8,128)} async-done(((f32[1024,1024]{1,0:T(8,128)}), f32[8,1024]{1,0:T(8,128)}) %reduce-scatter.15.cloned.1.call-update) | async-done | bytes 32784 | tf_op jit(solution)/shard_map/reduce_scatter | solution.py:273
  1596.4 641.0 %reduce-scatter.21.cloned.1.call-done = f32[8,1024]{1,0:T(8,128)} async-done(((f32[1024,1024]{1,0:T(8,128)}), f32[8,1024]{1,0:T(8,128)}) %reduce-scatter.21.cloned.1.call-update) | async-done | bytes 32784 | tf_op jit(solution)/shard_map/reduce_scatter | solution.py:276
  2237.4 637.1 %reduce-scatter.19.cloned.1.call-done = f32[8,512]{1,0:T(8,128)} async-done(((f32[1024,512]{1,0:T(8,128)}), f32[8,512]{1,0:T(8,128)}) %reduce-scatter.19.cloned.1.call-update) | async-done | bytes 16400 | tf_op jit(solution)/shard_map/reduce_scatter | solution.py:275
  2874.5 638.7 %reduce-scatter.17.cloned.1.call-done = f32[8,512]{1,0:T(8,128)} async-done(((f32[1024,512]{1,0:T(8,128)}), f32[8,512]{1,0:T(8,128)}) %reduce-scatter.17.cloned.1.call-update) | async-done | bytes 16400 | tf_op jit(solution)/shard_map/reduce_scatter | solution.py:274
  3513.2 236.9 %reduce-scatter.25.cloned.1.call-done = f32[8,4608]{1,0:T(8,128)} async-done(((f32[1024,4608]{1,0:T(8,128)}), f32[8,4608]{1,0:T(8,128)}) %reduce-scatter.25.cloned.1.call-update) | async-done | bytes 147472 | tf_op jit(solution)/shard_map/reduce_scatter | solution.py:188
  3750.1 240.9 %reduce-scatter.23.cloned.1.call-done = f32[8,4608]{1,0:T(8,128)} async-done(((f32[1024,4608]{1,0:T(8,128)}), f32[8,4608]{1,0:T(8,128)}) %reduce-scatter.23.cloned.1.call-update) | async-done | bytes 147472 | tf_op jit(solution)/shard_map/reduce_scatter | solution.py:187
  (366 shorter events, 277.3 us)
Async XLA Ops:
  7.2 69.7 %all-gather.11.cloned.1.call-start = ((), (), s32[]{:S(2)}) async-start(), calls=%async_computation.8 | async-start | bytes 1056768 | tf_op jit(solution)/shard_map/all_gather | solution.py:90
  7.9 132.8 %all-gather.15.cloned.1.call-start = ((), (), s32[]{:S(2)}) async-start(), calls=%async_computation.10 | async-start | bytes 1056768 | tf_op jit(solution)/shard_map/all_gather | solution.py:89
  8.7 197.8 %all-gather.19.cloned.1.call-start = ((), (), s32[]{:S(2)}) async-start(), calls=%async_computation.12 | async-start | bytes 2113536 | tf_op jit(solution)/shard_map/all_gather | solution.py:88
  9.4 254.2 %all-gather.13.cloned.1.call-start = ((), (), s32[]{:S(2)}) async-start(), calls=%async_computation.9 | async-start | bytes 4456448 | tf_op jit(solution)/shard_map/all_gather | solution.py:110
  79.4 243.1 %all-gather.17.cloned.1.call-start = ((), (), s32[]{:S(2)}) async-start(), calls=%async_computation.11 | async-start | bytes 4456448 | tf_op jit(solution)/shard_map/all_gather | solution.py:109
  144.5 245.4 %all-gather.21.cloned.1.call-start = ((), (), s32[]{:S(2)}) async-start(), calls=%async_computation.13 | async-start | bytes 2113536 | tf_op jit(solution)/shard_map/all_gather | solution.py:91
  145.1 317.0 %all-gather.27.cloned.1.call-start = ((), (), s32[]{:S(2)}) async-start(), calls=%async_computation.23 | async-start | bytes 10567680 | tf_op jit(solution)/shard_map/all_gather | solution.py:152
  145.9 388.1 %all-gather.25.cloned.1.call-start = ((), (), s32[]{:S(2)}) async-start(), calls=%async_computation.15 | async-start | bytes 9510912 | tf_op jit(solution)/shard_map/all_gather | solution.py:151
  146.6 458.6 %all-gather.23.cloned.1.call-start = ((), (), s32[]{:S(2)}) async-start(), calls=%async_computation.14 | async-start | bytes 9510912 | tf_op jit(solution)/shard_map/all_gather | solution.py:150
  147.3 704.0 %reduce-scatter.13.cloned.1.call-start = ((), (), s32[]{:S(2)}) async-start(), calls=%async_computation.16 | async-start | bytes 4456448 | tf_op jit(solution)/shard_map/reduce_scatter | solution.py:246
  392.5 242.6 %copy-start.13 = (f32[256,1024]{1,0:T(8,128)}, f32[256,1024]{1,0:T(8,128)S(1)}, u32[]{:S(2)}) copy-start(f32[256,1024]{1,0:T(8,128)S(1)} %get-tuple-element.337) | copy-start | bytes 3145732
  775.9 156.2 %reduce-scatter.27.cloned.1.call-start = ((), (), s32[]{:S(2)}) async-start(), calls=%async_computation.24 | async-start | bytes 4456448
  792.7 803.7 %reduce-scatter.15.cloned.1.call-start = ((), (), s32[]{:S(2)}) async-start(), calls=%async_computation.17 | async-start | bytes 4227072 | tf_op jit(solution)/shard_map/reduce_scatter | solution.py:273
  798.1 1439.4 %reduce-scatter.21.cloned.1.call-start = ((), (), s32[]{:S(2)}) async-start(), calls=%async_computation.20 | async-start | bytes 4227072 | tf_op jit(solution)/shard_map/reduce_scatter | solution.py:276
  800.9 2073.6 %reduce-scatter.19.cloned.1.call-start = ((), (), s32[]{:S(2)}) async-start(), calls=%async_computation.19 | async-start | bytes 2113536 | tf_op jit(solution)/shard_map/reduce_scatter | solution.py:275
  854.2 2659.0 %reduce-scatter.17.cloned.1.call-start = ((), (), s32[]{:S(2)}) async-start(), calls=%async_computation.18 | async-start | bytes 2113536 | tf_op jit(solution)/shard_map/reduce_scatter | solution.py:274
  939.9 2810.2 %reduce-scatter.25.cloned.1.call-start = ((), (), s32[]{:S(2)}) async-start(), calls=%async_computation.22 | async-start | bytes 19021824 | tf_op jit(solution)/shard_map/reduce_scatter | solution.py:188
  949.5 3041.4 %reduce-scatter.23.cloned.1.call-start = ((), (), s32[]{:S(2)}) async-start(), calls=%async_computation.21 | async-start | bytes 19021824 | tf_op jit(solution)/shard_map/reduce_scatter | solution.py:187
  969.7 421.5 %copy-start.14 = (f32[256,1024]{1,0:T(8,128)S(1)}, f32[256,1024]{1,0:T(8,128)}, u32[]{:S(2)}) copy-start(f32[256,1024]{1,0:T(8,128)} %copy-done.13) | copy-start | bytes 3145732
  1370.0 14.9 collective-permute-start.11
  1371.3 14.9 collective-permute-start.10
  1374.2 4.3 collective-permute-start.12
  1375.5 23.5 collective-permute-start.9
  1376.9 27.2 collective-permute-start.8
  1378.5 27.0 collective-permute-start.7
  1385.0 24.6 collective-permute-start.6
  1386.3 25.8 collective-permute-start.5
  1399.0 18.1 collective-permute-start.4
  1404.2 13.0 collective-permute-start.3
  1405.5 11.7 collective-permute-start.2
  1409.6 7.6 collective-permute-start.1
  1412.1 6.5 collective-permute-start
  (86 other events, 2282.0 us)
Sparse Core Ops, SparseCore 0:
  10.8 65.9 all-gather.10
  79.6 61.0 all-gather.14
  143.7 62.7 all-gather.18
  208.4 55.1 all-gather.12
  265.5 56.9 all-gather.16
  325.4 64.4 all-gather.20
  393.0 69.0 all-gather.26
  465.0 68.9 all-gather.24
  536.8 68.3 all-gather.22
  776.0 75.2 reduce-scatter.12
  855.0 76.9 reduce-scatter.26
  934.8 661.5 reduce-scatter.14
  1599.5 637.9 reduce-scatter.20
  2240.2 634.2 reduce-scatter.18
  2877.4 635.7 reduce-scatter.16
  3518.9 231.1 reduce-scatter.24
  3756.7 234.2 reduce-scatter.22
where the time goes:
time: 4000 us
  waiting for transfers between devices  3100 us (78%)
  blocking collectives  474 us (12%)
  matrix products  211 us (5%)
  local copies, waits for them, and re-layouts  115 us (3%)
  other arithmetic  47.5 us (1%)
    reduce_scatter x1, waiting for transfers between devices, local(): lax.psum_scatter(grad_out, ('dp', 'ctx'), scatter_dimension=0, tiled=True)  641 us
    reduce_scatter x1, waiting for transfers between devices, local(): lax.psum_scatter(grad_key, ('dp', 'ctx'), scatter_dimension=0, tiled=True)  639 us
    reduce_scatter x1, waiting for transfers between devices, local(): lax.psum_scatter(grad_value, ('dp', 'ctx'), scatter_dimension=0, tiled=True)  637 us
    unnamed x1, blocking collectives  400 us
    reduce_scatter x1, waiting for transfers between devices, local(): lax.psum_scatter(grad_gate, ('dp', 'ctx'), scatter_dimension=0, tiled=True)  241 us
    reduce_scatter x1, waiting for transfers between devices, local(): lax.psum_scatter(grad_up, ('dp', 'ctx'), scatter_dimension=0, tiled=True)  237 us
    unnamed x31, waiting for transfers between devices  88.1 us
  transfers between devices with their start and end apart: 30, of which 19 were waited for; matrix products, arithmetic and copies ran while one was open for 15% of the time, Pallas kernels for 0%

commit v1 on v0

v1 whole, which is shorter than its diff:
```python
import functools

import jax
import jax.numpy as jnp
from jax import lax
from jax.experimental import pallas as pl
from jax.experimental.pallas import tpu as pltpu
from jax.sharding import PartitionSpec as P

MESH = pl.DeviceIdType.MESH
BF = jnp.bfloat16
F32 = jnp.float32

D = 1024
HDIM = 64
HEADS = 8
ROWS = 256
SEQ = 2048
PADDED = 40
HALF = 64 * PADDED
EPSILON = 1e-05
THETA_BASE = 1000000.0
LOG2E = 1.4426950408889634
VMEM_MOST = 60 * 1024 * 1024


def params(**more):
    return pltpu.CompilerParams(vmem_limit_bytes=VMEM_MOST, **more)


def vmem():
    return pl.BlockSpec(memory_space=pltpu.VMEM)


def hbm():
    return pl.BlockSpec(memory_space=pl.ANY)


def dot(left, right):
    return lax.dot_general(left, right, (((1,), (0,)), ((), ())), preferred_element_type=F32)


def dot_rows(left, right):
    return lax.dot_general(left, right, (((0,), (0,)), ((), ())), preferred_element_type=F32)


def dot_cols(left, right):
    return lax.dot_general(left, right, (((1,), (1,)), ((), ())), preferred_element_type=F32)


def place():
    dp, ctx = lax.axis_index("dp"), lax.axis_index("ctx")
    return {"y": dp // 2, "c": dp % 2, "z": ctx // 4, "x": ctx % 4}


def device(at, **moved):
    spot = dict(at)
    spot.update(moved)
    return (spot["y"] * 2 + spot["c"], spot["z"] * 4 + spot["x"])


def beside(at, dim, by):
    return device(at, **{dim: (at[dim] + by) % 4})


def greet(at, dims="xyz", core=True):
    barrier = pltpu.get_barrier_semaphore()
    count = 0
    for dim in dims:
        for by in (1, 3):
            pl.semaphore_signal(barrier, inc=1, device_id=beside(at, dim, by), device_id_type=MESH)
            count += 1
    if core:
        pl.semaphore_signal(barrier, inc=1, device_id=device(at, c=1 - at["c"]), device_id_type=MESH)
        count += 1
    pl.semaphore_wait(barrier, count)


ORDERS = (("x", "z", "y"), ("y", "x", "z"), ("z", "y", "x"))


class Layout:
    def __init__(self, kind, order, columns):
        self.kind, self.order, self.columns = kind, order, columns

    def index(self, at, full, fixed=None, half=None):
        spot = dict(at)
        if fixed:
            spot.update(fixed)
        ids = {d: (slice(None) if d in full else spot[d]) for d in "xyz"}
        c = {"own": at["c"], "both": slice(None), "none": None}[self.kind]
        out = [ids["y"]] + ([] if c is None else [c]) + [ids["z"], ids["x"], slice(None)]
        if half is None:
            out.append(slice(None))
        else:
            out.append(pl.ds(half * (self.columns // 2), self.columns // 2))
        return tuple(out)


def gather_kernel(q_in, kv_in, o_in, g_in, u_in, d_in, q_out, kv_out, o_out, g_out, u_out, d_out, local_sem, core_send, core_recv, send, recv):
    at = place()
    c = at["c"]
    partner = device(at, c=1 - c)
    greet(at)
    layouts = [
        Layout("own", ORDERS[0], 1024), Layout("own", ORDERS[1], 1024), Layout("own", ORDERS[2], 1024),
        Layout("both", ORDERS[0], HALF), Layout("both", ORDERS[1], HALF), Layout("none", ORDERS[2], 1024),
    ]
    outs = [q_out, kv_out, o_out, g_out, u_out, d_out]
    here = (at["y"], c, at["z"], at["x"])
    down_here = (at["y"], at["z"], at["x"])

    core = []
    for i, (src, dst) in enumerate(((g_in, g_out), (u_in, u_out))):
        core.append(pltpu.make_async_remote_copy(
            src_ref=src.at[1 - c], dst_ref=dst.at[here], send_sem=core_send.at[i], recv_sem=core_recv.at[i],
            device_id=partner, device_id_type=MESH))
    for copy in core:
        copy.start()
    locals_ = [
        pltpu.make_async_copy(q_in, q_out.at[here], local_sem.at[0]),
        pltpu.make_async_copy(kv_in, kv_out.at[here], local_sem.at[1]),
        pltpu.make_async_copy(o_in, o_out.at[here], local_sem.at[2]),
        pltpu.make_async_copy(g_in.at[c], g_out.at[here], local_sem.at[3]),
        pltpu.make_async_copy(u_in.at[c], u_out.at[here], local_sem.at[4]),
        pltpu.make_async_copy(d_in, d_out.at[down_here], local_sem.at[5]),
    ]
    for copy in locals_:
        copy.start()
    for copy in locals_:
        copy.wait()

    sends = []

    def remote(i, stage, slot, index, to):
        copy = pltpu.make_async_remote_copy(
            src_ref=outs[i].at[index], dst_ref=outs[i].at[index], send_sem=send.at[i, stage, slot],
            recv_sem=recv.at[i, stage, slot], device_id=to, device_id_type=MESH)
        copy.start()
        sends.append(copy)

    def first(i, stage):
        lay = layouts[i]
        dim, full = lay.order[stage], lay.order[:stage]
        index = lay.index(at, full)
        remote(i, stage, 0, index, beside(at, dim, 1))
        remote(i, stage, 1, index, beside(at, dim, 3))

    def arrived(i, stage, slot, by, half):
        lay = layouts[i]
        dim, full = lay.order[stage], lay.order[:stage]
        index = lay.index(at, full, {dim: (at[dim] + by) % 4}, half)
        pltpu.make_async_remote_copy(
            src_ref=outs[i].at[index], dst_ref=outs[i].at[index], send_sem=send.at[i, stage, slot],
            recv_sem=recv.at[i, stage, slot], device_id=partner, device_id_type=MESH).wait_recv()

    def second(i, stage):
        lay = layouts[i]
        dim, full = lay.order[stage], lay.order[:stage]
        arrived(i, stage, 0, 3, None)
        remote(i, stage, 2, lay.index(at, full, {dim: (at[dim] + 3) % 4}, 0), beside(at, dim, 1))
        arrived(i, stage, 1, 1, None)
        remote(i, stage, 3, lay.index(at, full, {dim: (at[dim] + 1) % 4}, 1), beside(at, dim, 3))

    def last(i, stage):
        arrived(i, stage, 2, 2, 0)
        arrived(i, stage, 3, 2, 1)

    for i in range(3):
        first(i, 0)
    for copy in core:
        copy.wait_recv()
    for i in range(3, 6):
        first(i, 0)
    swaps = []
    for stage in range(3):
        for i in range(6):
            second(i, stage)
        for i in range(6):
            last(i, stage)
            if stage < 2:
                first(i, stage + 1)
            elif i < 3:
                index = (slice(None), c)
                copy = pltpu.make_async_remote_copy(
                    src_ref=outs[i].at[index], dst_ref=outs[i].at[index], send_sem=core_send.at[2 + i],
                    recv_sem=core_recv.at[2 + i], device_id=partner, device_id_type=MESH)
                copy.start()
                swaps.append(copy)
    for copy in core:
        copy.wait_send()
    for i in range(3):
        index = (slice(None), 1 - c)
        pltpu.make_async_remote_copy(
            src_ref=outs[i].at[index], dst_ref=outs[i].at[index], send_sem=core_send.at[2 + i],
            recv_sem=core_recv.at[2 + i], device_id=partner, device_id_type=MESH).wait_recv()
    for copy in swaps:
        copy.wait_send()
    for copy in sends:
        copy.wait_send()


def gather(*shards):
    attn = jax.ShapeDtypeStruct((4, 2, 4, 4, 8, D), BF)
    wide = jax.ShapeDtypeStruct((4, 2, 4, 4, 8, HALF), BF)
    down = jax.ShapeDtypeStruct((4, 4, 4, PADDED, D), BF)
    dma = pltpu.SemaphoreType.DMA
    return pl.pallas_call(
        gather_kernel,
        out_shape=(attn, attn, attn, wide, wide, down),
        in_specs=[hbm()] * 6,
        out_specs=[hbm()] * 6,
        scratch_shapes=[dma((6,)), dma((5,)), dma((5,)), dma((6, 3, 4)), dma((6, 3, 4))],
        compiler_params=params(collective_id=0, has_side_effects=True),
    )(*shards)


def scatter_kernel(*refs):
    grads, gains_in = refs[:6], refs[6]
    q_fin, kv_fin, o_fin, g_fin, u_fin, d_fin, gains_out = refs[7:14]
    fins = [q_fin, kv_fin, o_fin, g_fin, u_fin, d_fin]
    core_bufs = refs[14:17]
    recvs = [refs[17 + 6 * i : 23 + 6 * i] for i in range(6)]
    gain_bufs = refs[53]
    wide_fin = refs[54:56]
    core_send, core_recv, send, recv, fin_send, fin_recv, gain_send, gain_recv = refs[56:64]
    at = place()
    c = at["c"]
    partner = device(at, c=1 - c)
    greet(at)
    layouts = [
        Layout("own", ORDERS[0], 1024), Layout("own", ORDERS[1], 1024), Layout("own", ORDERS[2], 1024),
        Layout("both", ORDERS[0], HALF), Layout("both", ORDERS[1], HALF), Layout("none", ORDERS[2], 1024),
    ]
    waits = []

    for i in range(3):
        copy = pltpu.make_async_remote_copy(
            src_ref=grads[i].at[:, 1 - c], dst_ref=core_bufs[i], send_sem=core_send.at[i], recv_sem=core_recv.at[i],
            device_id=partner, device_id_type=MESH)
        copy.start()
        waits.append(copy)

    def remote(src, dst, i, stage, slot, to):
        copy = pltpu.make_async_remote_copy(
            src_ref=src, dst_ref=dst, send_sem=send.at[i, stage, slot], recv_sem=recv.at[i, stage, slot],
            device_id=to, device_id_type=MESH)
        copy.start()
        waits.append(copy)

    def arrived(dst, i, stage, slot):
        pltpu.make_async_remote_copy(
            src_ref=dst, dst_ref=dst, send_sem=send.at[i, stage, slot], recv_sem=recv.at[i, stage, slot],
            device_id=partner, device_id_type=MESH).wait_recv()

    def bufs(i, stage):
        lay = layouts[i]
        half = lay.columns // 2
        both = recvs[i][2 * stage]
        near = recvs[i][2 * stage + 1]
        return both.at[0], both.at[1], near.at[0], near.at[1], half

    def chunk(i, stage, by, half=None):
        lay = layouts[i]
        dim, full = lay.order[stage], lay.order[stage + 1 :]
        return lay.index(at, full, {dim: (at[dim] + by) % 4}, half)

    def first(i, stage):
        dim = layouts[i].order[stage]
        h0, h1, _, _, _ = bufs(i, stage)
        remote(grads[i].at[chunk(i, stage, 2, 0)], h0, i, stage, 0, beside(at, dim, 1))
        remote(grads[i].at[chunk(i, stage, 2, 1)], h1, i, stage, 1, beside(at, dim, 3))

    def add(target, others, lead):
        def body(ids):
            spot = tuple(ids)
            total = target[spot].astype(F32)
            for other in others:
                total = total + other[spot].astype(F32)
            target[spot] = total.astype(target.dtype)
        loop(lead, body)

    def loop(lead, body):
        count = 1
        for n in lead:
            count *= n
        if count == 1:
            body([0] * len(lead))
            return

        @pl.loop(0, count)
        def _(flat):
            ids = []
            for n in reversed(lead):
                ids.insert(0, flat % n)
                flat = flat // n
            body(ids)

    def leads(ref):
        return ref.shape[:-2]

    def second(i, stage):
        dim = layouts[i].order[stage]
        h0, h1, left, right, half = bufs(i, stage)
        arrived(h0, i, stage, 0)
        target = grads[i].at[chunk(i, stage, 1, 0)]
        add(target, [h0], leads(h0))
        remote(grads[i].at[chunk(i, stage, 1)], left, i, stage, 2, beside(at, dim, 1))
        arrived(h1, i, stage, 1)
        target = grads[i].at[chunk(i, stage, 3, 1)]
        add(target, [h1], leads(h1))
        remote(grads[i].at[chunk(i, stage, 3)], right, i, stage, 3, beside(at, dim, 3))

    def last(i, stage):
        _, _, left, right, _ = bufs(i, stage)
        arrived(left, i, stage, 2)
        arrived(right, i, stage, 3)
        target = grads[i].at[chunk(i, stage, 0)]
        if stage < 2:
            add(target, [left, right], leads(left))
            return
        fin = fins[i] if i not in (3, 4) else wide_fin[i - 3]

        def body(ids):
            spot = tuple(ids)
            fin[spot] = target[spot].astype(F32) + left[spot].astype(F32) + right[spot].astype(F32)
        loop(leads(left), body)

    order = (3, 4, 5, 0, 1, 2)
    for i in (3, 4, 5):
        first(i, 0)
    for i in range(3):
        waits[i].wait_recv()
        add(grads[i].at[:, c], [core_bufs[i]], leads(core_bufs[i]))
        first(i, 0)

    def gain_stage(stage, dim):
        slots = gain_bufs.at[stage]
        p = at[dim]

        def move(slot, by, index):
            copy = pltpu.make_async_remote_copy(
                src_ref=slots.at[index], dst_ref=slots.at[index], send_sem=gain_send.at[stage, slot],
                recv_sem=gain_recv.at[stage, slot], device_id=beside(at, dim, by), device_id_type=MESH)
            copy.start()
            waits.append(copy)

        def here(slot, index):
            pltpu.make_async_remote_copy(
                src_ref=slots.at[index], dst_ref=slots.at[index], send_sem=gain_send.at[stage, slot],
                recv_sem=gain_recv.at[stage, slot], device_id=partner, device_id_type=MESH).wait_recv()

        move(0, 1, p)
        move(1, 3, p)
        here(0, (p + 3) % 4)
        move(2, 1, (p + 3) % 4)
        here(1, (p + 1) % 4)
        here(2, (p + 2) % 4)
        return slots[0] + slots[1] + slots[2] + slots[3]

    gain_bufs[0, at["x"]] = gains_in[...]
    total = None
    for stage in range(3):
        if stage > 0:
            gain_bufs[stage, at["xyz"[stage]]] = total
        total = gain_stage(stage, "xyz"[stage])
        for i in order:
            second(i, stage)
        for i in order:
            last(i, stage)
            if stage < 2:
                first(i, stage + 1)
    gain_bufs[3, c] = total
    spot = gain_bufs.at[3, c]
    copy = pltpu.make_async_remote_copy(
        src_ref=spot, dst_ref=spot, send_sem=gain_send.at[3, 0], recv_sem=gain_recv.at[3, 0], device_id=partner,
        device_id_type=MESH)
    copy.start()
    swaps = []
    for k in range(2):
        swap = pltpu.make_async_remote_copy(
            src_ref=wide_fin[k].at[1 - c], dst_ref=fins[3 + k].at[c], send_sem=fin_send.at[k], recv_sem=fin_recv.at[k],
            device_id=partner, device_id_type=MESH)
        swap.start()
        swaps.append(swap)
        fins[3 + k][c] = wide_fin[k][c]
    copy.wait()
    gains_out[...] = gain_bufs[3, 0] + gain_bufs[3, 1]
    for k in range(2):
        swaps[k].wait_send()
        pltpu.make_async_remote_copy(
            src_ref=fins[3 + k].at[1 - c], dst_ref=fins[3 + k].at[1 - c], send_sem=fin_send.at[k], recv_sem=fin_recv.at[k],
            device_id=partner, device_id_type=MESH).wait_recv()
    for copy in waits:
        copy.wait_send()


def chunk_shapes(kind, order, rows, columns):
    shapes = []
    for stage in range(3):
        left = order[stage + 1 :]
        lead = ([4] if "y" in left else []) + ([2] if kind == "both" else [])
        lead += [4] if "z" in left else []
        lead += [4] if "x" in left else []
        shapes.append(tuple(lead))
    out = []
    for lead in shapes:
        out.append(pltpu.VMEM((2, *lead, rows, columns // 2), BF))
        out.append(pltpu.VMEM((2, *lead, rows, columns), BF))
    return out


def scatter(q, kv, o, g, u, d, gains):
    small = jax.ShapeDtypeStruct((8, D), F32)
    wide = jax.ShapeDtypeStruct((2, 8, HALF), F32)
    down = jax.ShapeDtypeStruct((PADDED, D), F32)
    dma = pltpu.SemaphoreType.DMA
    scratch = [pltpu.VMEM((4, 4, 4, 8, D), BF)] * 3
    for order in ORDERS:
        scratch += chunk_shapes("own", order, 8, D)
    scratch += chunk_shapes("both", ORDERS[0], 8, HALF)
    scratch += chunk_shapes("both", ORDERS[1], 8, HALF)
    scratch += chunk_shapes("none", ORDERS[2], PADDED, D)
    scratch += [pltpu.VMEM((4, 4, *gains.shape), F32)]
    scratch += [pltpu.VMEM((2, 8, HALF), F32)] * 2
    scratch += [dma((3,)), dma((3,)), dma((6, 3, 4)), dma((6, 3, 4)), dma((2,)), dma((2,)), dma((4, 3)), dma((4, 3))]
    return pl.pallas_call(
        scatter_kernel,
        out_shape=(small, small, small, wide, wide, down, jax.ShapeDtypeStruct(gains.shape, F32)),
        in_specs=[vmem()] * 7,
        out_specs=[vmem()] * 7,
        scratch_shapes=scratch,
        compiler_params=params(collective_id=1, has_side_effects=True),
    )(q, kv, o, g, u, d, gains)


def swap_kernel(count, *refs):
    ins, outs = refs[:count], refs[count : 2 * count]
    send, recv, local = refs[2 * count :]
    dp, ctx = lax.axis_index("dp"), lax.axis_index("ctx")
    barrier = pltpu.get_barrier_semaphore()
    for step in range(1, 16):
        pl.semaphore_signal(barrier, inc=1, device_id=(dp, (ctx + step) % 16), device_id_type=MESH)
    copies = []
    for k in range(count):
        copy = pltpu.make_async_copy(ins[k].at[ctx], outs[k].at[ctx], local.at[k])
        copy.start()
        copies.append(copy)
    pl.semaphore_wait(barrier, 15)
    for step in range(1, 16):
        to = (ctx + step) % 16
        for k in range(count):
            copy = pltpu.make_async_remote_copy(
                src_ref=ins[k].at[to], dst_ref=outs[k].at[ctx], send_sem=send.at[k, step], recv_sem=recv.at[k, step],
                device_id=(dp, to), device_id_type=MESH)
            copy.start()
            copies.append(copy)
    for copy in copies:
        copy.wait()


def swap(name, *arrays):
    count = len(arrays)
    dma = pltpu.SemaphoreType.DMA
    shape = jax.ShapeDtypeStruct((16, 128, 128), BF)
    return pl.pallas_call(
        functools.partial(swap_kernel, count),
        out_shape=(shape,) * count,
        in_specs=[hbm()] * count,
        out_specs=[hbm()] * count,
        scratch_shapes=[dma((count, 16)), dma((count, 16)), dma((count,))],
        compiler_params=params(collective_id=name, has_side_effects=True),
    )(*arrays)


def lanes(shape):
    return lax.broadcasted_iota(jnp.int32, shape, len(shape) - 1)


def norm(values, gain):
    factor = lax.rsqrt(jnp.mean(values * values, axis=-1, keepdims=True) + EPSILON)
    unit = values * factor
    return unit * gain, unit, factor


def split_dot(values, matrix):
    high = values.astype(BF)
    low = (values - high.astype(F32)).astype(BF)
    return dot(high, matrix) + dot(low, matrix)


def head_sum_matrix():
    rows = lax.broadcasted_iota(jnp.int32, (128, 128), 0) // HDIM
    return (rows == lanes((128, 128)) // HDIM).astype(BF)


def turn(values):
    low = lanes(values.shape) % HDIM < HDIM // 2
    ahead = pltpu.roll(values, 128 - HDIM // 2, 1)
    behind = pltpu.roll(values, HDIM // 2, 1)
    return jnp.where(low, -ahead, behind)


def project_kernel(x_ref, gain_ref, qgain_ref, kgain_ref, cos_ref, sin_ref, wq_ref, wkv_ref, h_ref, qraw_ref, kraw_ref, q_ref, kv_ref, low_ref):
    step = pl.program_id(0)

    @pl.when(step == 0)
    def _():
        normed, _, _ = norm(x_ref[...].astype(F32), gain_ref[...])
        low_ref[...] = normed.astype(BF)
        h_ref[...] = normed.astype(BF)

    low = low_ref[...]
    sums = head_sum_matrix()
    query = dot(low, wq_ref[...])
    key_value = dot(low, wkv_ref[...])
    qraw_ref[...] = query
    kraw_ref[...] = key_value
    cosine, sine = cos_ref[...], sin_ref[...]
    for h in range(2):
        def rotated(raw, gain):
            factor = lax.rsqrt(split_dot(raw * raw, sums) * (1.0 / HDIM) + EPSILON)
            normed = raw * factor * gain
            return normed * cosine + turn(normed) * sine
        raw = query[:, h * 128 : (h + 1) * 128]
        out = rotated(raw, qgain_ref[...]).astype(BF)
        raw = key_value[:, h * 128 : (h + 1) * 128]
        pair = jnp.where(lanes(raw.shape) < HDIM, rotated(raw, kgain_ref[...]), raw).astype(BF)
        for s in range(2):
            q_ref[s, h] = out[s * 128 : (s + 1) * 128]
            kv_ref[s, h] = pair[s * 128 : (s + 1) * 128]


def project(x, gain, qgain, kgain, cosine, sine, wq, wkv):
    full = lambda shape: pl.BlockSpec(shape, lambda i: (0,) * len(shape))
    wide = pl.BlockSpec((D, 256), lambda i: (0, i))
    raw = pl.BlockSpec((ROWS, 256), lambda i: (0, i))
    heads = pl.BlockSpec((2, 2, 128, 128), lambda i: (0, i, 0, 0))
    return pl.pallas_call(
        project_kernel,
        grid=(4,),
        out_shape=(
            jax.ShapeDtypeStruct((ROWS, D), BF), jax.ShapeDtypeStruct((ROWS, D), F32), jax.ShapeDtypeStruct((ROWS, D), F32),
            jax.ShapeDtypeStruct((2, 8, 128, 128), BF), jax.ShapeDtypeStruct((2, 8, 128, 128), BF),
        ),
        in_specs=[full((ROWS, D)), full((1, D)), full((1, 128)), full((1, 128)), full((ROWS, 128)), full((ROWS, 128)), wide, wide],
        out_specs=[full((ROWS, D)), raw, raw, heads, heads],
        scratch_shapes=[pltpu.VMEM((ROWS, D), BF)],
        compiler_params=params(),
    )(x, gain, qgain, kgain, cosine, sine, wq, wkv)


BLOCK = 256
SCALE2 = LOG2E * HDIM**-0.5


def attend_kernel(q_ref, kv_ref, segcol_ref, segrow_ref, o_ref, inv_ref):
    block = pl.program_id(0)
    low_lane = lanes((BLOCK, 128)) < HDIM
    q = q_ref[...]
    zero = jnp.zeros_like(q)
    stacked = jnp.concatenate([jnp.where(low_lane, q, zero), jnp.where(low_lane, pltpu.roll(q.astype(F32), HDIM, 1).astype(BF), zero)], axis=0)
    seg_q = segcol_ref[...]
    seg_q = jnp.concatenate([seg_q, seg_q], axis=0)

    def part(j, total, diagonal):
        rows = pl.ds(pl.multiple_of(j * BLOCK, BLOCK), BLOCK)
        kv = kv_ref[rows, :]
        scores = dot_cols(stacked, kv)
        allowed = seg_q == segrow_ref[:, rows]
        if diagonal:
            query = lax.broadcasted_iota(jnp.int32, (2 * BLOCK, BLOCK), 0) % BLOCK
            allowed = allowed & (query >= lanes((2 * BLOCK, BLOCK)))
        weights = jnp.where(allowed, jnp.exp2(scores * SCALE2), 0.0).astype(BF)
        values = jnp.where(low_lane, jnp.ones_like(kv), kv)
        return total + dot(weights, values)

    total = lax.fori_loop(0, block, lambda j, t: part(j, t, False), jnp.zeros((2 * BLOCK, 128), F32))
    total = part(block, total, True)
    sums = pltpu.roll(total, HDIM, 1)
    mixed = total / sums
    first = pltpu.roll(mixed[:BLOCK], HDIM, 1)
    o_ref[...] = jnp.where(low_lane, first, mixed[BLOCK:]).astype(BF)
    inv_ref[0:1, :] = 1.0 / jnp.transpose(total[:BLOCK])[0:1, :]
    inv_ref[1:2, :] = 1.0 / jnp.transpose(total[BLOCK:])[0:1, :]


def attend(q, kv, segcol, segrow):
    return pl.pallas_call(
        attend_kernel,
        grid=(SEQ // BLOCK,),
        out_shape=(jax.ShapeDtypeStruct((SEQ, 128), BF), jax.ShapeDtypeStruct((2, SEQ), F32)),
        in_specs=[
            pl.BlockSpec((BLOCK, 128), lambda i: (i, 0)), pl.BlockSpec((SEQ, 128), lambda i: (0, 0)),
            pl.BlockSpec((BLOCK, 1), lambda i: (i, 0)), pl.BlockSpec((1, SEQ), lambda i: (0, 0)),
        ],
        out_specs=[pl.BlockSpec((BLOCK, 128), lambda i: (i, 0)), pl.BlockSpec((2, BLOCK), lambda i: (0, i))],
        compiler_params=params(),
    )(q, kv, segcol, segrow)


def attend_back_kernel(q_ref, kv_ref, do_ref, o_ref, inv_ref, segcol_ref, segrow_ref, dq_ref, dkv_ref, qs, dos, drow, acc):
    block = pl.program_id(0)

    @pl.when(block == 0)
    def _():
        acc[...] = jnp.zeros_like(acc)
        low_lane = lanes((BLOCK, 128)) < HDIM
        pick = (lax.broadcasted_iota(jnp.int32, (8, 128), 0) == lanes((8, 128)) // HDIM).astype(BF)
        for i in range(SEQ // BLOCK):
            rows = slice(i * BLOCK, (i + 1) * BLOCK)
            q = q_ref[rows, :].astype(F32)
            do = do_ref[rows, :].astype(F32)
            qs[i, :BLOCK] = jnp.where(low_lane, q, 0.0).astype(BF)
            qs[i, BLOCK:] = jnp.where(low_lane, pltpu.roll(q, HDIM, 1), 0.0).astype(BF)
            dos[i, :BLOCK] = jnp.where(low_lane, 0.0, pltpu.roll(do, HDIM, 1)).astype(BF)
            dos[i, BLOCK:] = jnp.where(low_lane, 0.0, do).astype(BF)
            product = do * o_ref[rows, :].astype(F32)
            high = product.astype(BF)
            rest = (product - high.astype(F32)).astype(BF)
            sums = dot_cols(pick, high) + dot_cols(pick, rest)
            drow[i, 0:1, :BLOCK] = sums[0:1]
            drow[i, 0:1, BLOCK:] = sums[1:2]
            drow[i, 1:2, :BLOCK] = inv_ref[0:1, rows]
            drow[i, 1:2, BLOCK:] = inv_ref[1:2, rows]

    kv = kv_ref[...]
    seg_k = segcol_ref[...]

    def part(i, total, diagonal):
        queries, upstream = qs[i], dos[i]
        scores = dot_cols(kv, queries)
        slopes = dot_cols(kv, upstream)
        seg_q = segrow_ref[:, pl.ds(pl.multiple_of(i * BLOCK, BLOCK), BLOCK)]
        seg_q = jnp.concatenate([seg_q, seg_q], axis=1)
        allowed = seg_k == seg_q
        if diagonal:
            key = lax.broadcasted_iota(jnp.int32, (BLOCK, 2 * BLOCK), 0)
            allowed = allowed & (lanes((BLOCK, 2 * BLOCK)) % BLOCK >= key)
        weights = jnp.where(allowed, jnp.exp2(scores * SCALE2), 0.0) * drow[i, 1:2, :]
        change = (weights * (slopes - drow[i, 0:1, :])).astype(BF)
        total = total + dot(change, queries) * HDIM**-0.5 + dot(weights.astype(BF), upstream)
        acc[i] = acc[i] + dot_rows(change, kv)
        return total

    total = part(block, jnp.zeros((BLOCK, 128), F32), True)
    total = lax.fori_loop(block + 1, SEQ // BLOCK, lambda i, t: part(i, t, False), total)
    dkv_ref[...] = total.astype(BF)

    @pl.when(block == SEQ // BLOCK - 1)
    def _():
        low_lane = lanes((BLOCK, 128)) < HDIM
        for i in range(SEQ // BLOCK):
            rows = slice(i * BLOCK, (i + 1) * BLOCK)
            both = jnp.where(low_lane, acc[i, :BLOCK], pltpu.roll(acc[i, BLOCK:], HDIM, 1))
            dq_ref[rows, :] = (both * HDIM**-0.5).astype(BF)


def attend_back(q, kv, do, o, inv, segcol, segrow):
    full = lambda shape: pl.BlockSpec(shape, lambda i: (0,) * len(shape))
    blocks = SEQ // BLOCK
    return pl.pallas_call(
        attend_back_kernel,
        grid=(blocks,),
        out_shape=(jax.ShapeDtypeStruct((SEQ, 128), BF), jax.ShapeDtypeStruct((SEQ, 128), BF)),
        in_specs=[
            full((SEQ, 128)), pl.BlockSpec((BLOCK, 128), lambda i: (i, 0)), full((SEQ, 128)), full((SEQ, 128)), full((2, SEQ)),
            pl.BlockSpec((BLOCK, 1), lambda i: (i, 0)), full((1, SEQ)),
        ],
        out_specs=[full((SEQ, 128)), pl.BlockSpec((BLOCK, 128), lambda i: (i, 0))],
        scratch_shapes=[
            pltpu.VMEM((blocks, 2 * BLOCK, 128), BF), pltpu.VMEM((blocks, 2 * BLOCK, 128), BF),
            pltpu.VMEM((blocks, 2, 2 * BLOCK), F32), pltpu.VMEM((blocks, 2 * BLOCK, 128), F32),
        ],
        compiler_params=params(),
    )(q, kv, do, o, inv, segcol, segrow)


def heads_to_rows(ref):
    parts = [jnp.concatenate([ref[s * 8 + h] for h in range(8)], axis=1) for s in range(2)]
    return jnp.concatenate(parts, axis=0)


def middle_kernel(x_ref, o_ref, wo_ref, gain_ref, full_ref, x1_ref, h2_ref):
    attended = heads_to_rows(o_ref)
    full_ref[...] = attended
    residual = x_ref[...].astype(F32) + dot(attended, wo_ref[...])
    x1_ref[...] = residual
    normed, _, _ = norm(residual, gain_ref[...])
    h2_ref[...] = normed.astype(BF)


def middle(x, o, wo, gain):
    return pl.pallas_call(
        middle_kernel,
        out_shape=(
            jax.ShapeDtypeStruct((ROWS, D), BF), jax.ShapeDtypeStruct((ROWS, D), F32), jax.ShapeDtypeStruct((ROWS, D), BF),
        ),
        in_specs=[vmem()] * 4,
        out_specs=[vmem()] * 3,
        compiler_params=params(),
    )(x, o, wo, gain)


FF_BLOCK = 512


def feed_kernel(h_ref, m_ref, wg_ref, wu_ref, wd_ref, out_ref, back_ref, gg_ref, gu_ref, gd_ref, turned):
    step = pl.program_id(0)

    @pl.when(step == 0)
    def _():
        out_ref[...] = jnp.zeros_like(out_ref)
        back_ref[...] = jnp.zeros_like(back_ref)
        turned[...] = jnp.transpose(h_ref[...])

    low, upstream = h_ref[...], m_ref[...]
    gate = dot(low, wg_ref[...])
    up = dot(low, wu_ref[...])
    sig = jax.nn.sigmoid(gate)
    silu = gate * sig
    hidden = (silu * up).astype(BF)
    out_ref[...] += dot(hidden, wd_ref[...])
    slope = dot_cols(upstream, wd_ref[...])
    gate_grad = (slope * up * sig * (1.0 + gate * (1.0 - sig))).astype(BF)
    up_grad = (slope * silu).astype(BF)
    back_ref[...] += dot_cols(gate_grad, wg_ref[...]) + dot_cols(up_grad, wu_ref[...])
    gd_ref[...] = dot_rows(hidden, upstream).astype(BF)
    gg_ref[...] = dot(turned[...], gate_grad).astype(BF)
    gu_ref[...] = dot(turned[...], up_grad).astype(BF)


def feed(h, m, wg, wu, wd):
    full = lambda shape: pl.BlockSpec(shape, lambda i: (0,) * len(shape))
    wide = pl.BlockSpec((D, FF_BLOCK), lambda i: (0, i))
    tall = pl.BlockSpec((FF_BLOCK, D), lambda i: (i, 0))
    both = 2 * ROWS
    return pl.pallas_call(
        feed_kernel,
        grid=(HALF // FF_BLOCK,),
        out_shape=(
            jax.ShapeDtypeStruct((both, D), F32), jax.ShapeDtypeStruct((both, D), F32),
            jax.ShapeDtypeStruct((D, HALF), BF), jax.ShapeDtypeStruct((D, HALF), BF), jax.ShapeDtypeStruct((HALF, D), BF),
        ),
        in_specs=[full((both, D)), full((both, D)), wide, wide, tall],
        out_specs=[full((both, D)), full((both, D)), wide, wide, tall],
        scratch_shapes=[pltpu.VMEM((D, both), BF)],
        compiler_params=params(),
    )(h, m, wg, wu, wd)


def norm_back(upstream, gain, unit, factor):
    scaled = upstream * gain
    return factor * (scaled - unit * jnp.mean(scaled * unit, axis=-1, keepdims=True))


def after_kernel(x1_ref, out_ref, out_other, back_ref, back_other, m_ref, gain_ref, wo_ref, full_ref, y_ref, dx1_ref, do_ref, gout_ref, gain_out):
    residual = x1_ref[...]
    y_ref[...] = (residual + out_ref[...] + out_other[...]).astype(BF)
    gain = gain_ref[...]
    _, unit, factor = norm(residual, gain)
    upstream = back_ref[...] + back_other[...]
    gain_out[...] = jnp.sum(upstream * unit, axis=0, keepdims=True)
    dx1 = m_ref[...].astype(F32) + norm_back(upstream, gain, unit, factor)
    dx1_ref[...] = dx1
    da = dx1.astype(BF)
    gout_ref[...] = dot_rows(full_ref[...], da).astype(BF)
    do = dot_cols(da, wo_ref[...]).astype(BF)
    for s in range(2):
        for h in range(8):
            do_ref[s * 8 + h] = do[s * 128 : (s + 1) * 128, h * 128 : (h + 1) * 128]


def after(*arrays):
    return pl.pallas_call(
        after_kernel,
        out_shape=(
            jax.ShapeDtypeStruct((ROWS, D), BF), jax.ShapeDtypeStruct((ROWS, D), F32), jax.ShapeDtypeStruct((16, 128, 128), BF),
            jax.ShapeDtypeStruct((D, D), BF), jax.ShapeDtypeStruct((1, D), F32),
        ),
        in_specs=[vmem()] * 9,
        out_specs=[vmem()] * 5,
        compiler_params=params(),
    )(*arrays)


def final_kernel(x_ref, gain_ref, qgain_ref, kgain_ref, cos_ref, sin_ref, h_ref, qraw_ref, kraw_ref, dq_ref, dkv_ref, wq_ref, wkv_ref, dx1_ref,
                 y_ref, gq_ref, gkv_ref, gain_out, qgain_out, kgain_out, dq_full, dkv_full):
    cosine, sine = cos_ref[...], sin_ref[...]
    sums = head_sum_matrix()
    low_lane = lanes((ROWS, 128)) < HDIM
    qg = jnp.zeros((1, 128), F32)
    kg = jnp.zeros((1, 128), F32)

    def back(raw, upstream, gain):
        factor = lax.rsqrt(split_dot(raw * raw, sums) * (1.0 / HDIM) + EPSILON)
        unit = raw * factor
        turned = upstream * cosine - turn(upstream) * sine
        scaled = turned * gain
        mean = split_dot(scaled * unit, sums) * (1.0 / HDIM)
        return factor * (scaled - unit * mean), jnp.sum(turned * unit, axis=0, keepdims=True)

    for h in range(8):
        cols = slice(h * 128, (h + 1) * 128)
        upstream = jnp.concatenate([dq_ref[h], dq_ref[8 + h]], axis=0).astype(F32)
        pre, terms = back(qraw_ref[:, cols], upstream, qgain_ref[...])
        qg = qg + terms
        dq_full[:, cols] = pre.astype(BF)
        upstream = jnp.concatenate([dkv_ref[h], dkv_ref[8 + h]], axis=0).astype(F32)
        pre, terms = back(kraw_ref[:, cols], upstream, kgain_ref[...])
        kg = kg + terms
        dkv_full[:, cols] = jnp.where(low_lane, pre, upstream).astype(BF)
    qgain_out[...] = qg
    kgain_out[...] = kg
    dq, dkv, low = dq_full[...], dkv_full[...], h_ref[...]
    gq_ref[...] = dot_rows(low, dq).astype(BF)
    gkv_ref[...] = dot_rows(low, dkv).astype(BF)
    dh = dot_cols(dq, wq_ref[...]) + dot_cols(dkv, wkv_ref[...])
    _, unit, factor = norm(x_ref[...].astype(F32), gain_ref[...])
    gain_out[...] = jnp.sum(dh * unit, axis=0, keepdims=True)
    y_ref[...] = (dx1_ref[...] + norm_back(dh, gain_ref[...], unit, factor)).astype(BF)


def final(*arrays):
    row = lambda n: jax.ShapeDtypeStruct((1, n), F32)
    return pl.pallas_call(
        final_kernel,
        out_shape=(
            jax.ShapeDtypeStruct((ROWS, D), BF), jax.ShapeDtypeStruct((D, D), BF), jax.ShapeDtypeStruct((D, D), BF),
            row(D), row(128), row(128),
        ),
        in_specs=[vmem()] * 14,
        out_specs=[vmem()] * 6,
        scratch_shapes=[pltpu.VMEM((ROWS, D), BF), pltpu.VMEM((ROWS, D), BF)],
        compiler_params=params(),
    )(*arrays)


def tables(first_row):
    places = first_row + jnp.arange(128, dtype=jnp.int32)
    frequency = THETA_BASE ** (-jnp.arange(0, HDIM, 2, dtype=F32) / HDIM)
    angles = places.astype(F32)[:, None] * frequency[None, :]
    cosine, sine = jnp.tile(jnp.cos(angles), (2, 4)), jnp.tile(jnp.sin(angles), (2, 4))
    return cosine, sine


def pair_heads(wk, wv):
    rows = wk.shape[0]
    return jnp.concatenate([wk.reshape(rows, 8, 1, HDIM), wv.reshape(rows, 8, 1, HDIM)], axis=2).reshape(rows, D)


def by_core(w):
    w = w.reshape(8, 4, 2, 16, 36)
    w = jnp.pad(w, ((0, 0), (0, 0), (0, 0), (0, 0), (0, PADDED - 36)))
    return w.transpose(2, 0, 1, 3, 4).reshape(2, 8, HALF)


def from_core(w):
    w = w.reshape(2, 8, 4, 16, PADDED)[..., :36]
    return w.transpose(1, 2, 0, 3, 4).reshape(8, 4608)


def exchange(*arrays):
    pairs = [(i, i ^ 1) for i in range(8)]
    return [lax.ppermute(a, "dp", pairs) for a in arrays]


def local(block_in, segment_ids, attn_gain, w_query, w_key, w_value, query_gain, key_gain, w_out, ffn_gain, w_gate, w_up, w_down, out_grad):
    ctx = lax.axis_index("ctx")
    x = block_in.reshape(ROWS, D)
    m = out_grad.reshape(ROWS, D)
    cosine, sine = tables(ctx * 128)
    row = lambda v: v.reshape(1, -1)
    qgain, kgain = row(jnp.tile(query_gain, 2)), row(jnp.tile(key_gain, 2))
    seg = lax.dynamic_index_in_dim(segment_ids, ctx // 8, 0, keepdims=False)
    segcol, segrow = seg.reshape(SEQ, 1), seg.reshape(1, SEQ)

    wq, wkv, wo, wg, wu, wd = gather(
        w_query, pair_heads(w_key, w_value), w_out, by_core(w_gate), by_core(w_up), jnp.pad(w_down, ((0, PADDED - 36), (0, 0))))
    wq, wkv, wo = wq.reshape(D, D), wkv.reshape(D, D), wo.reshape(D, D)
    wg, wu, wd = wg.reshape(D, HALF), wu.reshape(D, HALF), wd.reshape(HALF, D)

    h1, qraw, kraw, q, kv = project(x, row(attn_gain), qgain, kgain, cosine, sine, wq, wkv)
    q, kv = swap(2, q.reshape(16, 128, 128), kv.reshape(16, 128, 128))
    q, kv = q.reshape(SEQ, 128), kv.reshape(SEQ, 128)
    o, inv = attend(q, kv, segcol, segrow)
    (o_rows,) = swap(3, o.reshape(16, 128, 128))
    attended, x1, h2 = middle(x, o_rows, wo, row(ffn_gain))
    h2_other, m_other = exchange(h2, m)
    out, back, gg, gu, gd = feed(
        jnp.concatenate([h2, h2_other]), jnp.concatenate([m, m_other]), wg, wu, wd)
    out_other, back_other = exchange(out[ROWS:], back[ROWS:])
    y, dx1, do, gout, ffn_terms = after(
        x1, out[:ROWS], out_other, back[:ROWS], back_other, m, row(ffn_gain), wo, attended)
    (do_seq,) = swap(4, do)
    dq, dkv = attend_back(q, kv, do_seq.reshape(SEQ, 128), o, inv, segcol, segrow)
    dq, dkv = swap(5, dq.reshape(16, 128, 128), dkv.reshape(16, 128, 128))
    y_in, gq, gkv, attn_terms, qterms, kterms = final(
        x, row(attn_gain), qgain, kgain, cosine, sine, h1, qraw, kraw, dq, dkv, wq, wkv, dx1)
    terms = jnp.concatenate([attn_terms, ffn_terms, qterms, kterms, jnp.zeros((1, 768), F32)], axis=1).reshape(24, 128)
    small = lambda a: a.reshape(4, 2, 4, 4, 8, D)
    gq, gkv, gout, gg, gu, gd, terms = scatter(
        small(gq), small(gkv), small(gout), gg.reshape(4, 2, 4, 4, 8, HALF), gu.reshape(4, 2, 4, 4, 8, HALF),
        gd.reshape(4, 4, 4, PADDED, D), terms)
    terms = terms.reshape(-1)
    gkv = gkv.reshape(8, 8, 2, HDIM)
    return (
        y.reshape(2, 128, D), y_in.reshape(2, 128, D), gq, gkv[:, :, 0].reshape(8, 512), gkv[:, :, 1].reshape(8, 512), gout,
        from_core(gg), from_core(gu), gd[:36], terms[:D], terms[2 * D : 2 * D + 64] + terms[2 * D + 64 : 2 * D + 128],
        terms[2 * D + 128 : 2 * D + 192], terms[D : 2 * D],
    )


def solution(mesh):
    both = P(("dp", "ctx"), None)
    acts = P("dp", "ctx", None)
    return jax.shard_map(
        local,
        mesh=mesh,
        in_specs=(acts, P("dp", None), P(), both, both, both, P(), P(), both, P(), both, both, both, acts),
        out_specs=(acts, acts, both, both, both, both, both, both, both, P(), P(), P(), P()),
        check_vma=False,
    )
```

time: 4000 us -> 391 us (0.10)
  waiting for transfers between devices: 3100 us -> 3.56 us
  blocking collectives: 474 us -> 0 us
  Pallas kernels: 0 us -> 350 us
  matrix products: 211 us -> 0 us
  local copies, waits for them, and re-layouts: 115 us -> 30.3 us
  other arithmetic: 47.5 us -> 3.72 us
    reduce_scatter x7 -> x0, waiting for transfers between devices: 2520 us -> none  [the longest x1 641 us: local(): lax.psum_scatter(grad_out, ('dp', 'ctx'), scatter_dimension=0, tiled=True)]
    all_gather x9 -> x0, waiting for transfers between devices: 495 us -> none  [the longest x1 69.4 us: local(): lax.all_gather(w_down, ('dp', 'ctx'), axis=0, tiled=True)]
    unnamed x1 -> x0, blocking collectives: 400 us -> none
    pallas_call x0 -> x13, Pallas kernels: none -> 350 us  [the longest x1 101 us: scatter(): pl.pallas_call(scatter_kernel, out_shape=(small, small, small, wide, wide...]
    dot_general x35 -> x0, matrix products: 211 us -> none  [the longest x7 38.6 us: across_rows(): lax.dot_general(left, right, (((0,), (0,)), ((), ())), preferred_element_...]
    unnamed x31 -> x0, waiting for transfers between devices: 88.1 us -> none
    psum x1 -> x0, blocking collectives: 73.8 us -> none  [local(): lax.psum((jnp.sum(attn_terms, axis=0), jnp.sum(query_gain_terms, axis=(0,...]
    unnamed x127 -> x39, local copies, waits for them, and re-layouts: 63.2 us -> 5.66 us
  transfers between devices with their start and end apart: 30 -> 4, of which waited for: 19 -> 3; matrix products, arithmetic and copies ran while one was open for 15% -> 4% of each run, Pallas kernels for 0% -> 38%
where the time goes in v1:
time: 391 us; the launch traced here: 390 us
  Pallas kernels  350 us (90%)
  local copies, waits for them, and re-layouts  30.3 us (8%)
    pallas_call x1, Pallas kernels, scatter(): pl.pallas_call(scatter_kernel, out_shape=(small, small, small, wide, wide...  101 us
    pallas_call x1, Pallas kernels, gather(): pl.pallas_call(gather_kernel, out_shape=(attn, attn, attn, wide, wide, do...  89.6 us
    pallas_call x4, Pallas kernels, swap(): pl.pallas_call(functools.partial(swap_kernel, count), out_shape=(shape,)...  57.7 us
    pallas_call x1, Pallas kernels, feed(): pl.pallas_call(feed_kernel, grid=(HALF // FF_BLOCK,), out_shape=(jax.Shap...  31.5 us
    pallas_call x1, Pallas kernels, attend_back(): pl.pallas_call(attend_back_kernel, grid=(blocks,), out_shape=(jax.ShapeDt...  25.6 us
    pallas_call x1, Pallas kernels, attend(): pl.pallas_call(attend_kernel, grid=(SEQ // BLOCK,), out_shape=(jax.ShapeD...  18.9 us
    pallas_call x1, Pallas kernels, final(): pl.pallas_call(final_kernel, out_shape=(jax.ShapeDtypeStruct((ROWS, D), B...  9.45 us
  transfers between devices with their start and end apart: 4, of which 3 were waited for; matrix products, arithmetic and copies ran while one was open for 4% of the time, Pallas kernels for 38%

profile of v1, /device:TPU:0, one launch (start us, length us, event | category | flops | bytes accessed | tf_op | source)
XLA Modules:
  0.0 389.6 jit_solution(13013272415581145268)
XLA Ops:
  4.1 0.8 reshape.264
  7.5 1.5 reshape.227
  9.1 1.0 reshape.228.g_in
  10.8 1.0 reshape.230.u_in
  11.8 1.3 copy.39.segcol_ref
  13.7 89.6 %shard_map.237 = (bf16[4,2,4,4,8,1024]{5,4,3,2,1,0:T(8,128)(2,1)}, bf16[4,2,4,4,8,1024]{5,4,3,2,1,0:T(8,128)(2,1)}, bf16[4,2,4,4,8,1024]{5,4,3,2,1,0:T(8,128)(2,...) custom-call(bf16[8,1024]{1,0:T(8,128)(2,1)} %q_in.1, ...), custom_call_target="tpu_custom_call" | custom-call | tf_op jit(solution)/shard_map/pallas_call | solution.py:208
  103.4 6.9 %shard_map.238 = (bf16[256,1024]{1,0:T(8,128)(2,1)}, f32[256,1024]{1,0:T(8,128)}, f32[256,1024]{1,0:T(8,128)}, bf16[2,8,128,128]{3,2,1,0:T(8,128)(2,1)}, bf16[2,8,128,128]{3,2,1,0:T(8,128)(2,1)}) custom-call(bf16[256,1024]{1,0:T(8,128)(2,1)} %bitcast.77, f32[1,1024]{1,0:T(1,128)} %bitcast.104, f32[1,128]{1,0:T(1,128)} %reshape_tile.6.qgain_ref, ...), custom_call_target="tpu_custom_call" | custom-call | tf_op jit(solution)/shard_map/pallas_call | solution.py:539
  110.3 16.0 %shard_map.239 = (bf16[16,128,128]{2,1,0:T(8,128)(2,1)}, bf16[16,128,128]{2,1,0:T(8,128)(2,1)}) custom-call(bf16[16,128,128]{2,1,0:T(8,128)(2,1)} %bitcast.94, bf16[16,128,128]{2,1,0:T(8,128)(2,1)} %bitcast.95), custom_call_target="tpu_custom_call" | custom-call | tf_op jit(solution)/shard_map/pallas_call | solution.py:466
  126.9 18.9 %shard_map.240 = (bf16[2048,128]{1,0:T(8,128)(2,1)}, f32[2,2048]{1,0:T(2,128)}) custom-call(bf16[2048,128]{1,0:T(8,128)(2,1)} %bitcast.82, bf16[2048,128]{1,0:T(8,128)(2,1)} %bitcast.84, s32[2048,1]{1,0:T(8,128)} %copy.39.segcol_ref, s32[1,2048]{1,0:T(1,128)} %constant_dynamic-slice_fusion.segrow_ref), custom_call_target="tpu_custom_call" | custom-call | tf_op jit(solution)/shard_map/pallas_call | solution.py:589
  145.8 10.9 %shard_map.241.o_ref = bf16[16,128,128]{2,1,0:T(8,128)(2,1)} custom-call(bf16[16,128,128]{2,1,0:T(8,128)(2,1)} %bitcast.80), custom_call_target="tpu_custom_call" | custom-call | tf_op jit(solution)/shard_map/pallas_call | solution.py:466
  156.7 3.8 shard_map.242
  160.6 1.0 pad_maximum_fusion.1.m_ref
  161.6 1.1 collective-permute-done
  162.7 1.1 pad_maximum_fusion.h_ref
  163.7 31.5 %shard_map.243 = (f32[512,1024]{1,0:T(8,128)}, f32[512,1024]{1,0:T(8,128)}, bf16[1024,2560]{1,0:T(8,128)(2,1)}, bf16[1024,2560]{1,0:T(8,128)(2,1)}, bf16[2560,1024]{1,0:T(8,128)(2,1)}) custom-call(bf16[512,1024]{1,0:T(8,128)(2,1)} %pad_maximum_fusion.h_ref, bf16[512,1024]{1,0:T(8,128)(2,1)} %pad_maximum_fusion.1.m_ref, bf16[1024,2560]{1,0:T(8,128)(2,1)} %bitcast.74, ...), custom_call_target="tpu_custom_call" | custom-call | tf_op jit(solution)/shard_map/pallas_call | solution.py:738
  195.3 2.8 fusion.1
  198.2 1.2 fusion
  199.8 1.0 collective-permute-done.2.out_other
  200.8 1.5 collective-permute-done.3.back_other
  202.3 1.1 copy-done.5
  203.3 6.2 %shard_map.244 = (bf16[256,1024]{1,0:T(8,128)(2,1)}, f32[256,1024]{1,0:T(8,128)}, bf16[16,128,128]{2,1,0:T(8,128)(2,1)}, bf16[1024,1024]{1,0:T(8,128)(2,1)}, f32[1,1024]{1,0:T(1,128)}) custom-call(f32[256,1024]{1,0:T(8,128)} %get-tuple-element.66.x1_ref, f32[256,1024]{1,0:T(8,128)} %get-tuple-element.108.out_ref, f32[256,1024]{1,0:T(8,128)} %copy-done.4, ...), custom_call_target="tpu_custom_call" | custom-call | tf_op jit(solution)/shard_map/pallas_call | solution.py:775
  209.5 12.3 %shard_map.245 = bf16[16,128,128]{2,1,0:T(8,128)(2,1)} custom-call(bf16[16,128,128]{2,1,0:T(8,128)(2,1)} %get-tuple-element.78.refs_0_), custom_call_target="tpu_custom_call" | custom-call | tf_op jit(solution)/shard_map/pallas_call | solution.py:466
  221.9 25.6 %shard_map.246 = (bf16[2048,128]{1,0:T(8,128)(2,1)}, bf16[2048,128]{1,0:T(8,128)(2,1)}) custom-call(bf16[2048,128]{1,0:T(8,128)(2,1)} %bitcast.83, bf16[2048,128]{1,0:T(8,128)(2,1)} %bitcast.85, bf16[2048,128]{1,0:T(8,128)(2,1)} %bitcast.81, bf16[2048,128]{1,0:T(8,128)(2,1)} %get-tuple-element.64.o_ref, f32[2,2048]{1,0:T(2,128)} %get-tuple-element.79.inv_ref, ...), custom_call_target="tpu_custom_call" | custom-call | tf_op jit(solution)/shard_map/pallas_call | solution.py:662
  247.5 18.5 %shard_map.247 = (bf16[16,128,128]{2,1,0:T(8,128)(2,1)}, bf16[16,128,128]{2,1,0:T(8,128)(2,1)}) custom-call(bf16[16,128,128]{2,1,0:T(8,128)(2,1)} %bitcast.92, bf16[16,128,128]{2,1,0:T(8,128)(2,1)} %bitcast.93), custom_call_target="tpu_custom_call" | custom-call | tf_op jit(solution)/shard_map/pallas_call | solution.py:466
  266.0 9.5 %shard_map.248 = (bf16[256,1024]{1,0:T(8,128)(2,1)}, bf16[1024,1024]{1,0:T(8,128)(2,1)}, bf16[1024,1024]{1,0:T(8,128)(2,1)}, f32[1,1024]{1,0:T(1,128)}, f32[1,128]{1,0:T(1,128)}, /*index=5*/f32[1,128]{1,0:T(1,128)}) custom-call(bf16[256,1024]{1,0:T(8,128)(2,1)} %bitcast.79, f32[1,1024]{1,0:T(1,128)} %bitcast.105, f32[1,128]{1,0:T(1,128)} %reshape_tile.6.qgain_ref, ...), custom_call_target="tpu_custom_call" | custom-call | tf_op jit(solution)/shard_map/pallas_call | solution.py:826
  278.1 100.6 %shard_map.249 = (f32[8,1024]{1,0:T(8,128)}, f32[8,1024]{1,0:T(8,128)}, f32[8,1024]{1,0:T(8,128)}, f32[2,8,2560]{2,1,0:T(8,128)}, f32[2,8,2560]{2,1,0:T(8,128)}, /*index=5*/f32[40,1024]{1,0:T(8,128)}, f32[24,128]{1,0:T(8,128)}) custom-call(bf16[4,2,4,4,8,1024]{5,4,3,2,1,0:T(8,128)(2,1)} %bitcast.87, bf16[4,2,4,4,8,1024]{5,4,3,2,1,0:T(8,128)(2,1)} %bitcast.88, ...), custom_call_target="tpu_custom_call" | custom-call | tf_op jit(solution)/shard_map/pallas_call | solution.py:427
  378.7 1.3 slice_bitcast_fusion.2
  380.0 1.4 fusion.2
  381.4 0.9 reshape.257
  383.8 1.3 reshape.258
  385.2 0.9 reshape.259
  386.7 1.0 reshape.261
  (72 shorter events, 15.2 us)
Async XLA Ops:
  0.6 11.1 %copy-start = (s32[2,2048]{1,0:T(2,128)S(1)}, s32[2,2048]{1,0:T(2,128)}, u32[]{:S(2)}) copy-start(s32[2,2048]{1,0:T(2,128)} %param.15) | copy-start | bytes 49156
  0.7 9.4 %copy-start.10 = (bf16[8,4608]{1,0:T(8,128)(2,1)S(1)}, bf16[8,4608]{1,0:T(8,128)(2,1)}, u32[]{:S(2)}) copy-start(bf16[8,4608]{1,0:T(8,128)(2,1)} %param.25) | copy-start | bytes 221188
  0.7 159.9 %collective-permute-start.1 = (bf16[256,1024]{1,0:T(8,128)(2,1)}, bf16[256,1024]{1,0:T(8,128)(2,1)S(1)}, u32[]{:S(2)}, u32[]{:S(2)}) collective-permute-start(bf16[256,1024]{1,0:T(8,128)(2,1)} %bitcast.89), channel_id=1, source_target_pairs={{0,16},{16,0},{32,48},{48,32},{64,80},{80,64},{96,112},{112,96},{1... | collective-permute-start | bytes 1572872 | tf_op jit(solution)/shard_map/ppermute | solution.py:865
  6.6 6.4 %copy-start.9 = (bf16[36,1024]{1,0:T(8,128)(2,1)S(1)}, bf16[36,1024]{1,0:T(8,128)(2,1)}, u32[]{:S(2)}) copy-start(bf16[36,1024]{1,0:T(8,128)(2,1)} %param.26) | copy-start | bytes 221188
  145.8 14.8 %copy-start.3 = (bf16[2,128,1024]{2,1,0:T(8,128)(2,1)S(1)}, bf16[2,128,1024]{2,1,0:T(8,128)(2,1)}, u32[]{:S(2)}) copy-start(bf16[2,128,1024]{2,1,0:T(8,128)(2,1)} %param.27) | copy-start | bytes 1572868
  160.5 2.1 copy-start.6
  160.5 2.1 collective-permute-start
  195.3 3.0 copy-start.2
  198.1 2.7 collective-permute-start.2
  199.4 2.9 collective-permute-start.3
  200.8 1.5 copy-start.4
  202.3 1.1 copy-start.5
  266.0 10.2 %copy-start.14 = (f32[1,1024]{1,0:T(1,128)S(1)}, f32[1,1024]{1,0:T(1,128)}, u32[]{:S(2)}) copy-start(f32[1,1024]{1,0:T(1,128)} %get-tuple-element.93) | copy-start | bytes 12292
  277.5 0.6 copy-start.13
  378.7 7.5 %copy-start.8 = (f32[2,8,2560]{2,1,0:T(8,128)S(1)}, f32[2,8,2560]{2,1,0:T(8,128)}, u32[]{:S(2)}) copy-start(f32[2,8,2560]{2,1,0:T(8,128)} %get-tuple-element.100) | copy-start | bytes 491524
  385.2 2.5 copy-start.12
  385.2 3.1 copy-start.11
  385.2 3.7 copy-start.7
  385.2 4.3 %copy-start.1 = (s32[2,2048]{1,0:T(2,128)S(1)}, s32[2,2048]{1,0:T(2,128)}, u32[]{:S(2)}) copy-start(s32[2,2048]{1,0:T(2,128)} %param.15) | copy-start | bytes 49156

commit v2 on v0

v2 whole, which is shorter than its diff:
```python
import functools

import jax
import jax.numpy as jnp
from jax import lax
from jax.experimental import pallas as pl
from jax.experimental.pallas import tpu as pltpu
from jax.sharding import PartitionSpec as P

MESH = pl.DeviceIdType.MESH
BF = jnp.bfloat16
F32 = jnp.float32

D = 1024
HDIM = 64
HEADS = 8
ROWS = 256
SEQ = 2048
PADDED = 40
HALF = 64 * PADDED
EPSILON = 1e-05
THETA_BASE = 1000000.0
LOG2E = 1.4426950408889634
VMEM_MOST = 60 * 1024 * 1024


def params(**more):
    return pltpu.CompilerParams(vmem_limit_bytes=VMEM_MOST, **more)


def vmem():
    return pl.BlockSpec(memory_space=pltpu.VMEM)


def hbm():
    return pl.BlockSpec(memory_space=pl.ANY)


def dot(left, right):
    return lax.dot_general(left, right, (((1,), (0,)), ((), ())), preferred_element_type=F32)


def dot_rows(left, right):
    return lax.dot_general(left, right, (((0,), (0,)), ((), ())), preferred_element_type=F32)


def dot_cols(left, right):
    return lax.dot_general(left, right, (((1,), (1,)), ((), ())), preferred_element_type=F32)


def place():
    dp, ctx = lax.axis_index("dp"), lax.axis_index("ctx")
    return {"y": dp // 2, "c": dp % 2, "z": ctx // 4, "x": ctx % 4}


def device(at, **moved):
    spot = dict(at)
    spot.update(moved)
    return (spot["y"] * 2 + spot["c"], spot["z"] * 4 + spot["x"])


def beside(at, dim, by):
    return device(at, **{dim: (at[dim] + by) % 4})


ORDERS = (("x", "z", "y"), ("y", "x", "z"), ("z", "y", "x"))


class Layout:
    def __init__(self, kind, order, columns):
        self.kind, self.order, self.columns = kind, order, columns

    def index(self, at, full, fixed=None, half=None):
        spot = dict(at)
        if fixed:
            spot.update(fixed)
        ids = {d: (slice(None) if d in full else spot[d]) for d in "xyz"}
        c = {"own": at["c"], "both": slice(None), "none": None}[self.kind]
        out = [ids["y"]] + ([] if c is None else [c]) + [ids["z"], ids["x"], slice(None)]
        if half is None:
            out.append(slice(None))
        else:
            out.append(pl.ds(half * (self.columns // 2), self.columns // 2))
        return tuple(out)


class Gather:
    def __init__(self, at, arrays, layouts, send, recv):
        self.at, self.arrays, self.layouts, self.send, self.recv = at, arrays, layouts, send, recv
        self.started = []

    def copy(self, i, stage, slot, index, to):
        ref = self.arrays[i].at[index]
        return pltpu.make_async_remote_copy(
            src_ref=ref, dst_ref=ref, send_sem=self.send.at[i, stage, slot], recv_sem=self.recv.at[i, stage, slot],
            device_id=to, device_id_type=MESH)

    def start(self, i, stage, slot, index, to):
        copy = self.copy(i, stage, slot, index, to)
        copy.start()
        self.started.append(copy)

    def slab(self, i, stage, by, half=None):
        lay = self.layouts[i]
        dim, full = lay.order[stage], lay.order[:stage]
        return lay.index(self.at, full, {dim: (self.at[dim] + by) % 4}, half)

    def first(self, i, stage):
        dim = self.layouts[i].order[stage]
        self.start(i, stage, 0, self.slab(i, stage, 0), beside(self.at, dim, 1))
        self.start(i, stage, 1, self.slab(i, stage, 0), beside(self.at, dim, 3))

    def arrived(self, i, stage, slot, by, half):
        self.copy(i, stage, slot, self.slab(i, stage, by, half), beside(self.at, "x", 1)).wait_recv()

    def second(self, i, stage):
        dim = self.layouts[i].order[stage]
        self.arrived(i, stage, 0, 3, None)
        self.start(i, stage, 2, self.slab(i, stage, 3, 0), beside(self.at, dim, 1))
        self.arrived(i, stage, 1, 1, None)
        self.start(i, stage, 3, self.slab(i, stage, 1, 1), beside(self.at, dim, 3))

    def last(self, i, stage):
        self.arrived(i, stage, 2, 2, 0)
        self.arrived(i, stage, 3, 2, 1)


def layouts():
    return [
        Layout("own", ORDERS[0], D), Layout("own", ORDERS[1], D), Layout("own", ORDERS[2], D),
        Layout("both", ORDERS[0], HALF), Layout("both", ORDERS[1], HALF), Layout("none", ORDERS[2], D),
    ]


def lanes(shape):
    return lax.broadcasted_iota(jnp.int32, shape, len(shape) - 1)


def norm(values, gain):
    factor = lax.rsqrt(jnp.mean(values * values, axis=-1, keepdims=True) + EPSILON)
    unit = values * factor
    return unit * gain, unit, factor


def split_dot(values, matrix):
    high = values.astype(BF)
    low = (values - high.astype(F32)).astype(BF)
    return dot(high, matrix) + dot(low, matrix)


def head_sum_matrix():
    rows = lax.broadcasted_iota(jnp.int32, (128, 128), 0) // HDIM
    return (rows == lanes((128, 128)) // HDIM).astype(BF)


def turn(values):
    low = lanes(values.shape) % HDIM < HDIM // 2
    ahead = pltpu.roll(values, 128 - HDIM // 2, 1)
    behind = pltpu.roll(values, HDIM // 2, 1)
    return jnp.where(low, -ahead, behind)


BLOCK = 256
SCALE2 = LOG2E * HDIM**-0.5


def heads_to_rows(ref):
    parts = [jnp.concatenate([ref[s * 8 + h] for h in range(8)], axis=1) for s in range(2)]
    return jnp.concatenate(parts, axis=0)


def forward_kernel(x_ref, m_ref, gain_ref, qgain_ref, kgain_ref, fgain_ref, cos_ref, sin_ref, segcol_ref, segrow_ref,
                   q_in, kv_in, o_in, g_in, u_in, d_in,
                   wq_ref, wkv_ref, wo_ref, g_out, u_out, d_out, h_ref, qraw_ref, kraw_ref, qseq, kvseq, oseq, inv_ref, full_ref, x1_ref,
                   h2_ref, m2_ref,
                   wq8, wkv8, wo8, qown, kvown, orows,
                   local_sem, core_send, core_recv, send, recv, swap_send, swap_recv, swap_local):
    at = place()
    c = at["c"]
    dp, ctx = lax.axis_index("dp"), lax.axis_index("ctx")
    partner = device(at, c=1 - c)
    barrier = pltpu.get_barrier_semaphore()
    for to in (partner, beside(at, "y", 1), beside(at, "y", 3)):
        pl.semaphore_signal(barrier, inc=1, device_id=to, device_id_type=MESH)

    @pl.loop(1, 16)
    def _(step):
        pl.semaphore_signal(barrier, inc=1, device_id=(dp, (ctx + step) % 16), device_id_type=MESH)

    here = (at["y"], c, at["z"], at["x"])
    stays = [
        pltpu.make_async_copy(q_in, wq8.at[here], local_sem.at[0]),
        pltpu.make_async_copy(kv_in, wkv8.at[here], local_sem.at[1]),
        pltpu.make_async_copy(o_in, wo8.at[here], local_sem.at[2]),
        pltpu.make_async_copy(g_in.at[c], g_out.at[here], local_sem.at[3]),
        pltpu.make_async_copy(u_in.at[c], u_out.at[here], local_sem.at[4]),
        pltpu.make_async_copy(d_in, d_out.at[at["y"], at["z"], at["x"]], local_sem.at[5]),
    ]
    for copy in stays:
        copy.start()
    for copy in stays:
        copy.wait()
    pl.semaphore_wait(barrier, 18)

    ring = Gather(at, [wq8, wkv8, wo8, g_out, u_out, d_out], layouts(), send, recv)
    attn, feed_mats = (0, 1, 2), (3, 4, 5)

    def core_copy(slot, src, dst):
        return pltpu.make_async_remote_copy(
            src_ref=src, dst_ref=dst, send_sem=core_send.at[slot], recv_sem=core_recv.at[slot], device_id=partner,
            device_id_type=MESH)

    for i in attn:
        ring.first(i, 0)
    wide = [core_copy(0, g_in.at[1 - c], g_out.at[here]), core_copy(1, u_in.at[1 - c], u_out.at[here])]
    upstream_copy = core_copy(2, m_ref, m2_ref.at[1])
    for copy in wide:
        copy.start()
    upstream_copy.start()
    normed, _, _ = norm(x_ref[...].astype(F32), gain_ref[...])
    h_ref[...] = normed.astype(BF)
    m2_ref[0] = m_ref[...]
    for copy in wide:
        copy.wait_recv()
    for i in feed_mats:
        ring.first(i, 0)
    for i in attn:
        ring.second(i, 0)
    for i in attn:
        ring.last(i, 0)
        ring.first(i, 1)
    for i in feed_mats:
        ring.second(i, 0)
    for i in attn:
        ring.second(i, 1)
    for i in feed_mats:
        ring.last(i, 0)
        ring.first(i, 1)
    for i in attn:
        ring.last(i, 1)
        ring.first(i, 2)
    for i in feed_mats:
        ring.second(i, 1)
    for i in attn:
        ring.second(i, 2)
    for i in feed_mats:
        ring.last(i, 1)
        ring.first(i, 2)
    swaps = []
    eights = (wq8, wkv8, wo8)
    for i in attn:
        ring.last(i, 2)
        copy = core_copy(3 + i, eights[i].at[:, c], eights[i].at[:, c])
        copy.start()
        swaps.append(copy)

    def flatten(eight, flat, core):
        @pl.loop(0, 4)
        def _(y):
            rows = pl.ds(pl.multiple_of(y * 256 + core * 128, 128), 128)
            flat[rows, :] = eight[y, core].astype(F32).reshape(128, D).astype(BF)

    def other_rows(i):
        core_copy(3 + i, eights[i].at[:, 1 - c], eights[i].at[:, 1 - c]).wait_recv()

    flatten(wq8, wq_ref, c)
    flatten(wkv8, wkv_ref, c)
    other_rows(0)
    flatten(wq8, wq_ref, 1 - c)
    low = h_ref[...]
    query = dot(low, wq_ref[...])
    for h in range(8):
        qraw_ref[h] = query[:, h * 128 : (h + 1) * 128]
    other_rows(1)
    flatten(wkv8, wkv_ref, 1 - c)
    key_value = dot(low, wkv_ref[...])
    for h in range(8):
        kraw_ref[h] = key_value[:, h * 128 : (h + 1) * 128]

    sums = head_sum_matrix()
    cosine, sine = cos_ref[...], sin_ref[...]

    def rotated(raw, gain):
        factor = lax.rsqrt(split_dot(raw * raw, sums) * (1.0 / HDIM) + EPSILON)
        unit = raw * factor * gain
        return unit * cosine + turn(unit) * sine

    def swap_copy(k, src, dst, to, slot):
        return pltpu.make_async_remote_copy(
            src_ref=src, dst_ref=dst, send_sem=swap_send.at[k, to], recv_sem=swap_recv.at[k, slot], device_id=(dp, to),
            device_id_type=MESH)

    @pl.loop(0, 8)
    def _(step):
        h = (ctx + step) % 8
        raw = qraw_ref[h]
        qown[h] = rotated(raw, qgain_ref[...]).astype(BF)
        raw = kraw_ref[h]
        kvown[h] = jnp.where(lanes(raw.shape) < HDIM, rotated(raw, kgain_ref[...]), raw).astype(BF)
        for s in range(2):
            to = s * 8 + h
            rows = pl.ds(s * 128, 128)

            @pl.when(to != ctx)
            def _():
                swap_copy(0, kvown.at[h, rows], kvseq.at[ctx], to, ctx).start()
                swap_copy(1, qown.at[h, rows], qseq.at[ctx], to, ctx).start()

            @pl.when(to == ctx)
            def _():
                pltpu.make_async_copy(kvown.at[h, rows], kvseq.at[ctx], swap_local.at[0]).start()
                pltpu.make_async_copy(qown.at[h, rows], qseq.at[ctx], swap_local.at[1]).start()

    other_rows(2)
    flatten(wo8, wo_ref, c)
    flatten(wo8, wo_ref, 1 - c)

    low_lane = lanes((BLOCK, 128)) < HDIM

    def arrive(source):
        @pl.when(source != ctx)
        def _():
            swap_copy(0, kvseq.at[source], kvseq.at[source], source, source).wait_recv()
            swap_copy(1, qseq.at[source], qseq.at[source], source, source).wait_recv()

        @pl.when(source == ctx)
        def _():
            pltpu.make_async_copy(kvown.at[0, pl.ds(0, 128)], kvseq.at[ctx], swap_local.at[0]).wait()
            pltpu.make_async_copy(qown.at[0, pl.ds(0, 128)], qseq.at[ctx], swap_local.at[1]).wait()

    def queries(block):
        arrive(2 * block)
        arrive(2 * block + 1)
        q = qseq[pl.ds(2 * block, 2)].reshape(BLOCK, 128)
        zero = jnp.zeros_like(q)
        second = pltpu.roll(q.astype(F32), HDIM, 1).astype(BF)
        stacked = jnp.concatenate([jnp.where(low_lane, q, zero), jnp.where(low_lane, second, zero)], axis=0)
        rows = pl.ds(pl.multiple_of(block * BLOCK, BLOCK), BLOCK)
        seg_q = segcol_ref[rows, :]
        seg_q = jnp.concatenate([seg_q, seg_q], axis=0)

        def part(j, total, diagonal):
            kv = kvseq[pl.ds(2 * j, 2)].reshape(BLOCK, 128)
            scores = dot_cols(stacked, kv)
            allowed = seg_q == segrow_ref[:, pl.ds(pl.multiple_of(j * BLOCK, BLOCK), BLOCK)]
            if diagonal:
                query = lax.broadcasted_iota(jnp.int32, (2 * BLOCK, BLOCK), 0) % BLOCK
                allowed = allowed & (query >= lanes((2 * BLOCK, BLOCK)))
            weights = jnp.where(allowed, jnp.exp2(scores * SCALE2), 0.0).astype(BF)
            values = jnp.where(low_lane, jnp.ones_like(kv), kv)
            return total + dot(weights, values)

        total = lax.fori_loop(0, block, lambda j, t: part(j, t, False), jnp.zeros((2 * BLOCK, 128), F32))
        total = part(block, total, True)
        mixed = total / pltpu.roll(total, HDIM, 1)
        first = pltpu.roll(mixed[:BLOCK], HDIM, 1)
        oseq[pl.ds(2 * block, 2)] = jnp.where(low_lane, first, mixed[BLOCK:]).astype(BF).reshape(2, 128, 128)
        inv_ref[0:1, rows] = 1.0 / jnp.transpose(total[:BLOCK])[0:1, :]
        inv_ref[1:2, rows] = 1.0 / jnp.transpose(total[BLOCK:])[0:1, :]
        for k in range(2):
            to = 2 * block + k

            @pl.when(to != ctx)
            def _():
                swap_copy(2, oseq.at[to], orows.at[ctx], to, ctx).start()

            @pl.when(to == ctx)
            def _():
                pltpu.make_async_copy(oseq.at[to], orows.at[ctx], swap_local.at[2]).start()

    @pl.loop(0, 6)
    def _(block):
        queries(block)

    for i in feed_mats:
        ring.second(i, 2)

    @pl.loop(6, 8)
    def _(block):
        queries(block)

    @pl.loop(0, 16)
    def _(source):
        @pl.when(source != ctx)
        def _():
            swap_copy(2, orows.at[source], orows.at[source], source, source).wait_recv()

        @pl.when(source == ctx)
        def _():
            pltpu.make_async_copy(oseq.at[ctx], orows.at[ctx], swap_local.at[2]).wait()

    attended = heads_to_rows(orows)
    full_ref[...] = attended
    residual = x_ref[...].astype(F32) + dot(attended, wo_ref[...])
    x1_ref[...] = residual
    normed, _, _ = norm(residual, fgain_ref[...])
    h2_ref[0] = normed.astype(BF)
    mid_copy = core_copy(6, h2_ref.at[0], h2_ref.at[1])
    mid_copy.start()
    for i in feed_mats:
        ring.last(i, 2)

    @pl.loop(0, 16)
    def _(to):
        @pl.when(to != ctx)
        def _():
            swap_copy(0, kvown.at[0, pl.ds(0, 128)], kvseq.at[to], to, to).wait_send()
            swap_copy(1, qown.at[0, pl.ds(0, 128)], qseq.at[to], to, to).wait_send()
            swap_copy(2, oseq.at[to], orows.at[to], to, to).wait_send()

    for copy in wide + swaps:
        copy.wait_send()
    upstream_copy.wait()
    mid_copy.wait()
    for copy in ring.started:
        copy.wait_send()


def forward(*arrays):
    shape = jax.ShapeDtypeStruct
    dma = pltpu.SemaphoreType.DMA
    wide = shape((4, 2, 4, 4, 8, HALF), BF)
    return pl.pallas_call(
        forward_kernel,
        out_shape=(
            shape((D, D), BF), shape((D, D), BF), shape((D, D), BF), wide, wide, shape((4, 4, 4, PADDED, D), BF),
            shape((ROWS, D), BF), shape((8, ROWS, 128), F32), shape((8, ROWS, 128), F32), shape((16, 128, 128), BF),
            shape((16, 128, 128), BF), shape((16, 128, 128), BF), shape((2, SEQ), F32), shape((ROWS, D), BF), shape((ROWS, D), F32),
            shape((2, ROWS, D), BF), shape((2, ROWS, D), BF),
        ),
        in_specs=[vmem()] * 13 + [hbm()] * 3,
        out_specs=[vmem()] * 3 + [hbm()] * 3 + [vmem()] * 11,
        scratch_shapes=[pltpu.VMEM((4, 2, 4, 4, 8, D), BF)] * 3 + [pltpu.VMEM((8, ROWS, 128), BF)] * 2 + [pltpu.VMEM((16, 128, 128), BF)]
        + [dma((6,)), dma((7,)), dma((7,)), dma((6, 3, 4)), dma((6, 3, 4)), dma((3, 16)), dma((3, 16)), dma((3,))],
        compiler_params=params(collective_id=0, has_side_effects=True),
    )(*arrays)


FF_BLOCK = 512


def feed_kernel(h_ref, m_ref, wg_ref, wu_ref, wd_ref, out_ref, back_ref, gg_ref, gu_ref, gd_ref, turned):
    step = pl.program_id(0)

    @pl.when(step == 0)
    def _():
        out_ref[...] = jnp.zeros_like(out_ref)
        back_ref[...] = jnp.zeros_like(back_ref)
        turned[...] = jnp.transpose(h_ref[...])

    low, upstream = h_ref[...], m_ref[...]
    gate = dot(low, wg_ref[...])
    up = dot(low, wu_ref[...])
    sig = jax.nn.sigmoid(gate)
    silu = gate * sig
    hidden = (silu * up).astype(BF)
    out_ref[...] += dot(hidden, wd_ref[...])
    slope = dot_cols(upstream, wd_ref[...])
    gate_grad = (slope * up * sig * (1.0 + gate * (1.0 - sig))).astype(BF)
    up_grad = (slope * silu).astype(BF)
    back_ref[...] += dot_cols(gate_grad, wg_ref[...]) + dot_cols(up_grad, wu_ref[...])
    gd_ref[...] = dot_rows(hidden, upstream).astype(BF)
    gg_ref[...] = dot(turned[...], gate_grad).astype(BF)
    gu_ref[...] = dot(turned[...], up_grad).astype(BF)


def feed(h, m, wg, wu, wd):
    full = lambda shape: pl.BlockSpec(shape, lambda i: (0,) * len(shape))
    wide = pl.BlockSpec((D, FF_BLOCK), lambda i: (0, i))
    tall = pl.BlockSpec((FF_BLOCK, D), lambda i: (i, 0))
    both = 2 * ROWS
    return pl.pallas_call(
        feed_kernel,
        grid=(HALF // FF_BLOCK,),
        out_shape=(
            jax.ShapeDtypeStruct((both, D), F32), jax.ShapeDtypeStruct((both, D), F32),
            jax.ShapeDtypeStruct((D, HALF), BF), jax.ShapeDtypeStruct((D, HALF), BF), jax.ShapeDtypeStruct((HALF, D), BF),
        ),
        in_specs=[full((both, D)), full((both, D)), wide, wide, tall],
        out_specs=[full((both, D)), full((both, D)), wide, wide, tall],
        scratch_shapes=[pltpu.VMEM((D, both), BF)],
        compiler_params=params(),
    )(h, m, wg, wu, wd)


def norm_back(upstream, gain, unit, factor):
    scaled = upstream * gain
    return factor * (scaled - unit * jnp.mean(scaled * unit, axis=-1, keepdims=True))


class Scatter:
    def __init__(self, at, grads, layouts, bufs, own, fins, send, recv, load):
        self.at, self.grads, self.layouts, self.bufs, self.own, self.fins = at, grads, layouts, bufs, own, fins
        self.send, self.recv, self.load = send, recv, load
        self.started = []

    def copy(self, i, stage, slot, src, dst, to):
        return pltpu.make_async_remote_copy(
            src_ref=src, dst_ref=dst, send_sem=self.send.at[i, stage, slot], recv_sem=self.recv.at[i, stage, slot],
            device_id=to, device_id_type=MESH)

    def start(self, *args):
        copy = self.copy(*args)
        copy.start()
        self.started.append(copy)

    def arrived(self, i, stage, slot, dst):
        self.copy(i, stage, slot, dst, dst, beside(self.at, "x", 1)).wait_recv()

    def lanes(self, i, half):
        width = self.layouts[i].columns // 2
        return pl.ds(half * width, width)

    def source(self, i, stage, by, half):
        lay = self.layouts[i]
        dim, full = lay.order[stage], lay.order[stage + 1 :]
        if stage == 0:
            return self.grads[i].at[lay.index(self.at, full, {dim: (self.at[dim] + by) % 4}, half)]
        kept = [d for d in "yzx" if d in lay.order[stage:]]
        index = [slice(None) if d != dim else (self.at[dim] + by) % 4 for d in kept]
        if lay.kind == "both":
            index.insert(1 if "y" in kept else 0, slice(None))
        return self.bufs[i][2 * stage - 1].at[(0, *index, slice(None), self.lanes(i, half))]

    def parts(self, i, stage):
        halves, near = self.bufs[i][2 * stage], self.bufs[i][2 * stage + 1]
        row = (slice(None),) * (len(near.shape) - 2)
        return halves, near, lambda side, half: near.at[(side, *row, self.lanes(i, half))]

    def in_vmem(self, i, stage):
        return stage > 0 or self.own[i] is None

    def loads(self, i, stage, second):
        steps = ((0, 0, 0), (1, 0, 1)) if second else ((0, 1, 0), (1, 3, 1))
        return [
            pltpu.make_async_copy(self.source(i, stage, by, half), self.own[i].at[k], self.load.at[i, k]) for k, by, half in steps
        ]

    def first(self, i, stage):
        dim = self.layouts[i].order[stage]
        halves, near, part = self.parts(i, stage)
        ahead, behind = beside(self.at, dim, 1), beside(self.at, dim, 3)
        self.start(i, stage, 0, self.source(i, stage, 2, 0), halves.at[0], ahead)
        self.start(i, stage, 1, self.source(i, stage, 2, 1), halves.at[1], behind)
        self.start(i, stage, 2, self.source(i, stage, 1, 1), part(0, 1), ahead)
        self.start(i, stage, 3, self.source(i, stage, 3, 0), part(1, 0), behind)
        if not self.in_vmem(i, stage):
            for copy in self.loads(i, stage, False):
                copy.start()

    def second(self, i, stage):
        dim = self.layouts[i].order[stage]
        halves, near, part = self.parts(i, stage)
        for side, by in ((0, 1), (1, 3)):
            self.arrived(i, stage, side, halves.at[side])
            if self.in_vmem(i, stage):
                mine = self.source(i, stage, by, side)
            else:
                self.loads(i, stage, False)[side].wait()
                mine = self.own[i].at[side]
            add_into(halves.at[side], halves.at[side], mine)
            self.start(i, stage, 4 + side, halves.at[side], part(side, side), beside(self.at, dim, by))
        if not self.in_vmem(i, stage):
            for copy in self.loads(i, stage, True):
                copy.start()

    def last(self, i, stage):
        halves, near, part = self.parts(i, stage)
        self.arrived(i, stage, 2, part(0, 1))
        self.arrived(i, stage, 3, part(1, 0))
        self.arrived(i, stage, 4, part(0, 0))
        self.arrived(i, stage, 5, part(1, 1))
        for half in range(2):
            if self.in_vmem(i, stage):
                mine = self.source(i, stage, 0, half)
            else:
                self.loads(i, stage, True)[half].wait()
                mine = self.own[i].at[half]
            target = part(0, half)
            if stage == 2:
                target = self.fins[i].at[(slice(None),) * (len(self.fins[i].shape) - 1) + (self.lanes(i, half),)]
            add_into(target, part(0, half), part(1, half), mine)


def add_into(target, *terms):
    def body(spot):
        total = terms[0][spot].astype(F32)
        for term in terms[1:]:
            total = total + term[spot].astype(F32)
        target[spot] = total.astype(target.dtype)

    lead = target.shape[:-2]
    count = 1
    for n in lead:
        count *= n
    if count == 1:
        body((0,) * len(lead))
        return

    @pl.loop(0, count)
    def _(flat):
        spot = []
        for n in reversed(lead):
            spot.insert(0, flat % n)
            flat = flat // n
        body(tuple(spot))


def stage_shapes(lay, rows):
    shapes = []
    for stage in range(3):
        left = lay.order[stage + 1 :]
        lead = ([4] if "y" in left else []) + ([2] if lay.kind == "both" else [])
        lead += [4] * (("z" in left) + ("x" in left))
        shapes.append((2, *lead, rows, lay.columns // 2))
        shapes.append((2, *lead, rows, lay.columns))
    return shapes


def norm_back(upstream, gain, unit, factor):
    scaled = upstream * gain
    return factor * (scaled - unit * jnp.mean(scaled * unit, axis=-1, keepdims=True))


GAIN_ROWS = 24


def backward_kernel(*refs):
    (x_ref, m_ref, gain_ref, qgain_ref, kgain_ref, fgain_ref, cos_ref, sin_ref, segcol_ref, segrow_ref, x1_ref, out_hbm, back_hbm,
     full_ref, qseq, kvseq, oseq, inv_ref, h_ref, qraw_ref, kraw_ref, wo_hbm, wq_hbm, wkv_hbm, g_hbm, u_hbm, d_hbm) = refs[:27]
    (y_ref, yin_ref, q_fin, kv_fin, o_fin, g_fin, u_fin, d_fin, gains_out) = refs[27:36]
    (gq, gkv, go, out_own, back_own, out_other, back_other, do_own, do_seq, dq_own, dkv_own, dq_in, dkv_in, acc, dq_full, dkv_full,
     gains, gain_slots, wide_g, wide_u, first_mat, second_mat) = refs[36:58]
    cores = refs[58:61]
    own = [None, None, None, *refs[61:64]]
    bufs = [refs[64 + 6 * i : 70 + 6 * i] for i in range(6)]
    (core_send, core_recv, local_sem, send, recv, load_sem, swap_send, swap_recv, swap_local, gain_send, gain_recv) = refs[100:111]
    at = place()
    c = at["c"]
    dp, ctx = lax.axis_index("dp"), lax.axis_index("ctx")
    partner = device(at, c=1 - c)
    barrier = pltpu.get_barrier_semaphore()
    for to in (partner, beside(at, "y", 1), beside(at, "y", 3)):
        pl.semaphore_signal(barrier, inc=1, device_id=to, device_id_type=MESH)

    @pl.loop(1, 16)
    def _(step):
        pl.semaphore_signal(barrier, inc=1, device_id=(dp, (ctx + step) % 16), device_id_type=MESH)

    def core_copy(slot, src, dst):
        return pltpu.make_async_remote_copy(
            src_ref=src, dst_ref=dst, send_sem=core_send.at[slot], recv_sem=core_recv.at[slot], device_id=partner,
            device_id_type=MESH)

    rows_own, rows_other = pl.ds(0, ROWS), pl.ds(ROWS, ROWS)
    stays = [
        pltpu.make_async_copy(back_hbm.at[rows_own], back_own, local_sem.at[0]),
        pltpu.make_async_copy(out_hbm.at[rows_own], out_own, local_sem.at[1]),
        pltpu.make_async_copy(wo_hbm, first_mat, local_sem.at[2]),
        pltpu.make_async_copy(wkv_hbm, second_mat, local_sem.at[3]),
    ]
    for copy in stays:
        copy.start()
    pl.semaphore_wait(barrier, 18)
    swaps = [core_copy(0, back_hbm.at[rows_other], back_other), core_copy(1, out_hbm.at[rows_other], out_other)]
    for copy in swaps:
        copy.start()
    fins = [q_fin, kv_fin, o_fin, wide_g, wide_u, d_fin]
    ring = Scatter(at, [gq, gkv, go, g_hbm, u_hbm, d_hbm], layouts(), bufs, own, fins, send, recv, load_sem)
    attn, feed_mats = (0, 1, 2), (3, 4, 5)
    for i in feed_mats:
        ring.first(i, 0)

    for copy in stays:
        copy.wait()
    swaps[0].wait()
    residual = x1_ref[...]
    gain = fgain_ref[...]
    _, unit, factor = norm(residual, gain)
    upstream = back_own[...] + back_other[...]
    for k in range(8):
        gains[8 + k : 9 + k, :] = jnp.sum(upstream[:, k * 128 : (k + 1) * 128] * unit[:, k * 128 : (k + 1) * 128], axis=0, keepdims=True)
    dx1 = m_ref[...].astype(F32) + norm_back(upstream, gain, unit, factor)
    back_own[...] = dx1
    do = dot_cols(dx1.astype(BF), first_mat[...]).astype(BF)
    for s in range(2):
        for h in range(8):
            do_own[s * 8 + h] = do[s * 128 : (s + 1) * 128, h * 128 : (h + 1) * 128]
    query_mat = pltpu.make_async_copy(wq_hbm, first_mat, local_sem.at[4])
    query_mat.start()

    def swap_copy(k, src, dst, to, slot):
        return pltpu.make_async_remote_copy(
            src_ref=src, dst_ref=dst, send_sem=swap_send.at[k, to], recv_sem=swap_recv.at[k, slot], device_id=(dp, to),
            device_id_type=MESH)

    def swap_start(k, src, dst, to):
        @pl.when(to != ctx)
        def _():
            swap_copy(k, src.at[to], dst.at[ctx], to, ctx).start()

        @pl.when(to == ctx)
        def _():
            pltpu.make_async_copy(src.at[to], dst.at[ctx], swap_local.at[k]).start()

    def swap_wait(k, src, dst, source):
        @pl.when(source != ctx)
        def _():
            swap_copy(k, dst.at[source], dst.at[source], source, source).wait_recv()

        @pl.when(source == ctx)
        def _():
            pltpu.make_async_copy(src.at[ctx], dst.at[ctx], swap_local.at[k]).wait()

    @pl.loop(0, 16)
    def _(step):
        swap_start(0, do_own, do_seq, (ctx + step) % 16)

    acc[...] = jnp.zeros_like(acc)
    swaps[1].wait()
    y_ref[...] = (residual + out_own[...] + out_other[...]).astype(BF)

    def rows_gradient(grad, left, right):
        @pl.loop(0, 4)
        def _(y):
            cols = pl.ds(pl.multiple_of(y * 256, 256), 256)
            value = dot_rows(left[:, cols], right[...])
            grad[y] = value.reshape(2, 4, 4, 8, D).astype(BF)

    dq_full[...] = back_own[...].astype(BF)
    rows_gradient(go, full_ref, dq_full)
    swaps.append(core_copy(2, go.at[:, 1 - c], cores[2]))
    swaps[2].start()

    low_lane = lanes((BLOCK, 128)) < HDIM
    pick = (lax.broadcasted_iota(jnp.int32, (8, 128), 0) == lanes((8, 128)) // HDIM).astype(BF)

    def queries(block):
        swap_wait(0, do_own, do_seq, 2 * block)
        swap_wait(0, do_own, do_seq, 2 * block + 1)
        pair = pl.ds(2 * block, 2)
        rows = pl.ds(pl.multiple_of(block * BLOCK, BLOCK), BLOCK)
        q = qseq[pair].reshape(BLOCK, 128).astype(F32)
        do = do_seq[pair].reshape(BLOCK, 128).astype(F32)
        product = do * oseq[pair].reshape(BLOCK, 128).astype(F32)
        stacked = jnp.concatenate([jnp.where(low_lane, q, 0.0), jnp.where(low_lane, pltpu.roll(q, HDIM, 1), 0.0)], axis=0).astype(BF)
        above = jnp.concatenate([jnp.where(low_lane, 0.0, pltpu.roll(do, HDIM, 1)), jnp.where(low_lane, 0.0, do)], axis=0).astype(BF)
        high = product.astype(BF)
        rest = (product - high.astype(F32)).astype(BF)
        sums = dot_cols(pick, high) + dot_cols(pick, rest)
        row_dots = jnp.concatenate([sums[0:1], sums[1:2]], axis=1)
        inv = jnp.concatenate([inv_ref[0:1, rows], inv_ref[1:2, rows]], axis=1)
        seg_q = jnp.concatenate([segrow_ref[:, rows], segrow_ref[:, rows]], axis=1)

        def part(j, total, diagonal):
            kv = kvseq[pl.ds(2 * j, 2)].reshape(BLOCK, 128)
            scores = dot_cols(kv, stacked)
            slopes = dot_cols(kv, above)
            allowed = segcol_ref[pl.ds(pl.multiple_of(j * BLOCK, BLOCK), BLOCK), :] == seg_q
            if diagonal:
                key = lax.broadcasted_iota(jnp.int32, (BLOCK, 2 * BLOCK), 0)
                allowed = allowed & (lanes((BLOCK, 2 * BLOCK)) % BLOCK >= key)
            weights = jnp.where(allowed, jnp.exp2(scores * SCALE2), 0.0) * inv
            change = (weights * (slopes - row_dots)).astype(BF)
            acc[j] = acc[j] + dot(change, stacked) * HDIM**-0.5 + dot(weights.astype(BF), above)
            return total + dot_rows(change, kv)

        total = lax.fori_loop(0, block, lambda j, t: part(j, t, False), jnp.zeros((2 * BLOCK, 128), F32))
        total = part(block, total, True)
        both = jnp.where(low_lane, total[:BLOCK], pltpu.roll(total[BLOCK:], HDIM, 1)) * HDIM**-0.5
        dq_own[pair] = both.astype(BF).reshape(2, 128, 128)
        dkv_own[pair] = acc[block].astype(BF).reshape(2, 128, 128)
        for k in range(2):
            swap_start(1, dkv_own, dkv_in, 2 * block + k)
            swap_start(2, dq_own, dq_in, 2 * block + k)

    @pl.loop(0, 5)
    def _(step):
        queries(7 - step)

    for i in feed_mats:
        ring.second(i, 0)

    @pl.loop(5, 8)
    def _(step):
        queries(7 - step)

    cosine, sine = cos_ref[...], sin_ref[...]
    head_sums = head_sum_matrix()
    wide_lane = lanes((ROWS, 128)) < HDIM

    def head_back(raw, upstream, gain):
        factor = lax.rsqrt(split_dot(raw * raw, head_sums) * (1.0 / HDIM) + EPSILON)
        unit = raw * factor
        turned = upstream * cosine - turn(upstream) * sine
        scaled = turned * gain
        mean = split_dot(scaled * unit, head_sums) * (1.0 / HDIM)
        return factor * (scaled - unit * mean), jnp.sum(turned * unit, axis=0, keepdims=True)

    @pl.loop(0, 16)
    def _(source):
        swap_wait(1, dkv_own, dkv_in, source)
        swap_wait(2, dq_own, dq_in, source)

    qterms = jnp.zeros((1, 128), F32)
    kterms = jnp.zeros((1, 128), F32)
    for h in range(8):
        cols = slice(h * 128, (h + 1) * 128)
        upstream = jnp.concatenate([dq_in[h], dq_in[8 + h]], axis=0).astype(F32)
        pre, terms = head_back(qraw_ref[h], upstream, qgain_ref[...])
        qterms = qterms + terms
        dq_full[:, cols] = pre.astype(BF)
        upstream = jnp.concatenate([dkv_in[h], dkv_in[8 + h]], axis=0).astype(F32)
        pre, terms = head_back(kraw_ref[h], upstream, kgain_ref[...])
        kterms = kterms + terms
        dkv_full[:, cols] = jnp.where(wide_lane, pre, upstream).astype(BF)
    gains[16:17, :] = qterms
    gains[17:18, :] = kterms
    gains[18:24, :] = jnp.zeros((6, 128), F32)
    rows_gradient(gq, h_ref, dq_full)
    swaps.append(core_copy(3, gq.at[:, 1 - c], cores[0]))
    swaps[3].start()
    rows_gradient(gkv, h_ref, dkv_full)
    swaps.append(core_copy(4, gkv.at[:, 1 - c], cores[1]))
    swaps[4].start()
    for i in feed_mats:
        ring.last(i, 0)
        ring.first(i, 1)
    for slot, i in ((2, 2), (3, 0), (4, 1)):
        swaps[slot].wait_recv()
        mine = ring.grads[i].at[:, c]
        add_into(mine, mine, cores[i])
        ring.first(i, 0)

    query_mat.wait()
    dh = dot_cols(dq_full[...], first_mat[...]) + dot_cols(dkv_full[...], second_mat[...])
    gain = gain_ref[...]
    _, unit, factor = norm(x_ref[...].astype(F32), gain)
    for k in range(8):
        gains[k : k + 1, :] = jnp.sum(dh[:, k * 128 : (k + 1) * 128] * unit[:, k * 128 : (k + 1) * 128], axis=0, keepdims=True)
    yin_ref[...] = (back_own[...] + norm_back(dh, gain, unit, factor)).astype(BF)

    started = []

    def gain_copy(stage, slot, index, to):
        ref = gain_slots.at[stage, index]
        return pltpu.make_async_remote_copy(
            src_ref=ref, dst_ref=ref, send_sem=gain_send.at[stage, slot], recv_sem=gain_recv.at[stage, slot], device_id=to,
            device_id_type=MESH)

    def gain_start(stage, slot, index, to):
        copy = gain_copy(stage, slot, index, to)
        copy.start()
        started.append(copy)

    def gain_first(stage, total):
        dim = "xyz"[stage]
        p = at[dim]
        gain_slots[stage, p] = total
        gain_start(stage, 0, p, beside(at, dim, 1))
        gain_start(stage, 1, p, beside(at, dim, 3))

    def gain_second(stage):
        dim = "xyz"[stage]
        before = (at[dim] + 3) % 4
        gain_copy(stage, 0, before, partner).wait_recv()
        gain_start(stage, 2, before, beside(at, dim, 1))

    def gain_last(stage):
        dim = "xyz"[stage]
        gain_copy(stage, 1, (at[dim] + 1) % 4, partner).wait_recv()
        gain_copy(stage, 2, (at[dim] + 2) % 4, partner).wait_recv()
        return gain_slots[stage, 0] + gain_slots[stage, 1] + gain_slots[stage, 2] + gain_slots[stage, 3]

    gain_first(0, gains[...])
    for i in attn:
        ring.second(i, 0)
    gain_second(0)
    for i in feed_mats:
        ring.second(i, 1)
    for i in attn:
        ring.last(i, 0)
        ring.first(i, 1)
    gain_first(1, gain_last(0))
    for i in feed_mats:
        ring.last(i, 1)
        ring.first(i, 2)
    for i in attn:
        ring.second(i, 1)
    gain_second(1)
    for i in feed_mats:
        ring.second(i, 2)
    for i in attn:
        ring.last(i, 1)
        ring.first(i, 2)
    gain_first(2, gain_last(1))
    finals = []
    for i in feed_mats:
        ring.last(i, 2)
        if i < 5:
            wide, fin = ring.fins[i], (g_fin, u_fin)[i - 3]
            finals.append(core_copy(2 + i, wide.at[1 - c], fin.at[c]))
            finals[-1].start()
            fin[c] = wide[c]
    for i in attn:
        ring.second(i, 2)
    gain_second(2)
    for i in attn:
        ring.last(i, 2)
    gain_slots[3, c] = gain_last(2)
    finals.append(core_copy(7, gain_slots.at[3, c], gain_slots.at[3, c]))
    finals[-1].start()
    for slot, fin in ((5, g_fin), (6, u_fin)):
        core_copy(slot, fin.at[1 - c], fin.at[1 - c]).wait_recv()
    core_copy(7, gain_slots.at[3, 1 - c], gain_slots.at[3, 1 - c]).wait_recv()
    gains_out[...] = gain_slots[3, 0] + gain_slots[3, 1]

    @pl.loop(0, 16)
    def _(to):
        @pl.when(to != ctx)
        def _():
            swap_copy(0, do_own.at[to], do_seq.at[to], to, to).wait_send()
            swap_copy(1, dkv_own.at[to], dkv_in.at[to], to, to).wait_send()
            swap_copy(2, dq_own.at[to], dq_in.at[to], to, to).wait_send()

    for copy in swaps[2:] + finals + started + ring.started:
        copy.wait_send()


def backward(*arrays):
    shape = jax.ShapeDtypeStruct
    dma = pltpu.SemaphoreType.DMA
    small = shape((8, D), F32)
    wide = shape((2, 8, HALF), F32)
    block = pltpu.VMEM((16, 128, 128), BF)
    own = pltpu.VMEM((ROWS, D), F32)
    scratch = [pltpu.VMEM((4, 2, 4, 4, 8, D), BF)] * 3 + [own] * 4 + [block] * 6
    scratch += [pltpu.VMEM((SEQ // BLOCK, BLOCK, 128), F32)] + [pltpu.VMEM((ROWS, D), BF)] * 2
    scratch += [pltpu.VMEM((GAIN_ROWS, 128), F32), pltpu.VMEM((4, 4, GAIN_ROWS, 128), F32)] + [pltpu.VMEM((2, 8, HALF), F32)] * 2
    scratch += [pltpu.VMEM((D, D), BF)] * 2 + [pltpu.VMEM((4, 4, 4, 8, D), BF)] * 3
    lays = layouts()
    shapes = [stage_shapes(lay, PADDED if lay.kind == "none" else 8) for lay in lays]
    scratch += [pltpu.VMEM(shapes[i][0], BF) for i in (3, 4, 5)]
    for group in shapes:
        scratch += [pltpu.VMEM(s, BF) for s in group]
    scratch += [
        dma((8,)), dma((8,)), dma((5,)), dma((6, 3, 6)), dma((6, 3, 6)), dma((6, 2)), dma((3, 16)), dma((3, 16)), dma((3,)), dma((3, 3)),
        dma((3, 3)),
    ]
    return pl.pallas_call(
        backward_kernel,
        out_shape=(
            shape((ROWS, D), BF), shape((ROWS, D), BF), small, small, small, wide, wide, shape((PADDED, D), F32),
            shape((GAIN_ROWS, 128), F32),
        ),
        in_specs=[vmem()] * 11 + [hbm()] * 2 + [vmem()] * 8 + [hbm()] * 6,
        out_specs=[vmem()] * 9,
        scratch_shapes=scratch,
        compiler_params=params(collective_id=1, has_side_effects=True),
    )(*arrays)


def tables(first_row):
    places = first_row + jnp.arange(128, dtype=jnp.int32)
    frequency = THETA_BASE ** (-jnp.arange(0, HDIM, 2, dtype=F32) / HDIM)
    angles = places.astype(F32)[:, None] * frequency[None, :]
    cosine, sine = jnp.tile(jnp.cos(angles), (2, 4)), jnp.tile(jnp.sin(angles), (2, 4))
    return cosine, sine


def pair_heads(wk, wv):
    rows = wk.shape[0]
    return jnp.concatenate([wk.reshape(rows, 8, 1, HDIM), wv.reshape(rows, 8, 1, HDIM)], axis=2).reshape(rows, D)


def by_core(w):
    w = w.reshape(8, 4, 2, 16, 36)
    w = jnp.pad(w, ((0, 0), (0, 0), (0, 0), (0, 0), (0, PADDED - 36)))
    return w.transpose(2, 0, 1, 3, 4).reshape(2, 8, HALF)


def from_core(w):
    w = w.reshape(2, 8, 4, 16, PADDED)[..., :36]
    return w.transpose(1, 2, 0, 3, 4).reshape(8, 4608)


def local(block_in, segment_ids, attn_gain, w_query, w_key, w_value, query_gain, key_gain, w_out, ffn_gain, w_gate, w_up, w_down, out_grad):
    ctx = lax.axis_index("ctx")
    x = block_in.reshape(ROWS, D)
    m = out_grad.reshape(ROWS, D)
    cosine, sine = tables(ctx * 128)
    row = lambda v: v.reshape(1, -1)
    qgain, kgain = row(jnp.tile(query_gain, 2)), row(jnp.tile(key_gain, 2))
    seg = lax.dynamic_index_in_dim(segment_ids, ctx // 8, 0, keepdims=False)
    segcol, segrow = seg.reshape(SEQ, 1), seg.reshape(1, SEQ)

    (wq, wkv, wo, wg, wu, wd, h1, qraw, kraw, q, kv, o, inv, attended, x1, h2, m2) = forward(
        x, m, row(attn_gain), qgain, kgain, row(ffn_gain), cosine, sine, segcol, segrow,
        w_query, pair_heads(w_key, w_value), w_out, by_core(w_gate), by_core(w_up), jnp.pad(w_down, ((0, PADDED - 36), (0, 0))))
    wg, wu, wd = wg.reshape(D, HALF), wu.reshape(D, HALF), wd.reshape(HALF, D)
    out, back, gg, gu, gd = feed(h2.reshape(2 * ROWS, D), m2.reshape(2 * ROWS, D), wg, wu, wd)
    y, y_in, gq, gkv, gout, gg, gu, gd, terms = backward(
        x, m, row(attn_gain), qgain, kgain, row(ffn_gain), cosine, sine, segcol, segrow, x1, out, back, attended, q, kv, o, inv, h1,
        qraw, kraw, wo, wq, wkv, gg.reshape(4, 2, 4, 4, 8, HALF), gu.reshape(4, 2, 4, 4, 8, HALF), gd.reshape(4, 4, 4, PADDED, D))
    terms = terms.reshape(-1)
    gkv = gkv.reshape(8, 8, 2, HDIM)
    return (
        y.reshape(2, 128, D), y_in.reshape(2, 128, D), gq, gkv[:, :, 0].reshape(8, 512), gkv[:, :, 1].reshape(8, 512), gout,
        from_core(gg), from_core(gu), gd[:36], terms[:D], terms[2 * D : 2 * D + 64] + terms[2 * D + 64 : 2 * D + 128],
        terms[2 * D + 128 : 2 * D + 192], terms[D : 2 * D],
    )


def solution(mesh):
    both = P(("dp", "ctx"), None)
    acts = P("dp", "ctx", None)
    return jax.shard_map(
        local,
        mesh=mesh,
        in_specs=(acts, P("dp", None), P(), both, both, both, P(), P(), both, P(), both, both, both, acts),
        out_specs=(acts, acts, both, both, both, both, both, both, both, P(), P(), P(), P()),
        check_vma=False,
    )
```

time: 4000 us -> 328 us (0.08)
  waiting for transfers between devices: 3100 us -> 0 us
  blocking collectives: 474 us -> 0 us
  Pallas kernels: 0 us -> 297 us
  matrix products: 211 us -> 0 us
  local copies, waits for them, and re-layouts: 115 us -> 26.8 us
  other arithmetic: 47.5 us -> 1.62 us
    reduce_scatter x7 -> x0, waiting for transfers between devices: 2520 us -> none  [the longest x1 641 us: local(): lax.psum_scatter(grad_out, ('dp', 'ctx'), scatter_dimension=0, tiled=True)]
    all_gather x9 -> x0, waiting for transfers between devices: 495 us -> none  [the longest x1 69.4 us: local(): lax.all_gather(w_down, ('dp', 'ctx'), axis=0, tiled=True)]
    unnamed x1 -> x0, blocking collectives: 400 us -> none
    pallas_call x0 -> x3, Pallas kernels: none -> 297 us  [the longest x1 146 us: backward(): pl.pallas_call(backward_kernel, out_shape=(shape((ROWS, D), BF), shape((R...]
    dot_general x35 -> x0, matrix products: 211 us -> none  [the longest x7 38.6 us: across_rows(): lax.dot_general(left, right, (((0,), (0,)), ((), ())), preferred_element_...]
    unnamed x31 -> x0, waiting for transfers between devices: 88.1 us -> none
    psum x1 -> x0, blocking collectives: 73.8 us -> none  [local(): lax.psum((jnp.sum(attn_terms, axis=0), jnp.sum(query_gain_terms, axis=(0,...]
    unnamed x127 -> x19, local copies, waits for them, and re-layouts: 63.2 us -> 3.53 us
  transfers between devices with their start and end apart: 30 -> 0, of which waited for: 19 -> 0; matrix products, arithmetic and copies ran while one was open for 15% -> 0% of each run, Pallas kernels for 0% -> 0%
where the time goes in v2:
time: 328 us; the launch traced here: 326 us
  Pallas kernels  297 us (91%)
  local copies, waits for them, and re-layouts  26.8 us (8%)
    pallas_call x1, Pallas kernels, backward(): pl.pallas_call(backward_kernel, out_shape=(shape((ROWS, D), BF), shape((R...  146 us
    pallas_call x1, Pallas kernels, forward(): pl.pallas_call(forward_kernel, out_shape=(shape((D, D), BF), shape((D, D)...  119 us
    pallas_call x1, Pallas kernels, feed(): pl.pallas_call(feed_kernel, grid=(HALF // FF_BLOCK,), out_shape=(jax.Shap...  31.7 us

profile of v2, /device:TPU:0, one launch (start us, length us, event | category | flops | bytes accessed | tf_op | source)
XLA Modules:
  0.0 326.4 jit_solution(15409593610718076456)
XLA Ops:
  0.7 0.7 tile.12
  1.4 0.6 reshape_tile.6.qgain_ref.refs_3_
  2.0 0.7 tile.13
  3.2 0.6 constant_dynamic-slice_fusion.segrow_ref.refs_9_
  4.0 0.8 reshape.211
  4.8 0.8 reshape.212
  5.6 0.7 reshape.190.kv_in
  6.3 1.5 pad.13.d_in
  7.9 0.8 copy.41.sin_ref.refs_7_
  8.7 0.8 copy.40.cos_ref.refs_6_
  9.5 1.5 reshape.191
  11.1 1.0 reshape.192.g_in
  12.1 1.5 reshape.193
  13.7 1.0 reshape.194.u_in
  14.7 1.3 copy.42.segcol_ref.refs_8_
  16.0 119.4 %shard_map.237 = (bf16[1024,1024]{1,0:T(8,128)(2,1)}, bf16[1024,1024]{1,0:T(8,128)(2,1)}, bf16[1024,1024]{1,0:T(8,128)(2,1)}, bf16[4,2,4,4,8,2560]{5,4,3,2,1,0:T...) custom-call(bf16[256,1024]{1,0:T(8,128)(2,1)} %bitcast.58, ...), custom_call_target="tpu_custom_call" | custom-call | tf_op jit(solution)/shard_map/pallas_call | solution.py:423
  135.4 31.7 %shard_map.238 = (f32[512,1024]{1,0:T(8,128)}, f32[512,1024]{1,0:T(8,128)}, bf16[1024,2560]{1,0:T(8,128)(2,1)}, bf16[1024,2560]{1,0:T(8,128)(2,1)}, bf16[2560,1024]{1,0:T(8,128)(2,1)}) custom-call(bf16[512,1024]{1,0:T(8,128)(2,1)} %bitcast.62, bf16[512,1024]{1,0:T(8,128)(2,1)} %bitcast.63, bf16[1024,2560]{1,0:T(8,128)(2,1)} %bitcast.52, ...), custom_call_target="tpu_custom_call" | custom-call | tf_op jit(solution)/shard_map/pallas_call | solution.py:472
  167.1 146.0 %shard_map.239 = (bf16[256,1024]{1,0:T(8,128)(2,1)}, bf16[256,1024]{1,0:T(8,128)(2,1)}, f32[8,1024]{1,0:T(8,128)}, f32[8,1024]{1,0:T(8,128)}, f32[8,1024]{1,0:T(...) custom-call(bf16[256,1024]{1,0:T(8,128)(2,1)} %bitcast.59, ...), custom_call_target="tpu_custom_call" | custom-call | tf_op jit(solution)/shard_map/pallas_call | solution.py:950
  313.1 1.4 fusion
  314.5 1.3 slice_bitcast_fusion.2
  315.8 0.9 reshape.205
  316.8 0.7 reshape_squeeze.7
  317.5 0.7 reshape_squeeze.6
  318.2 1.3 reshape.206
  319.6 1.0 reshape.207
  320.6 1.3 reshape.208
  322.0 1.0 reshape.209
  322.9 0.8 copy.60
  323.7 0.8 copy.61
  324.5 0.6 copy.62
  325.1 0.6 copy.63
  325.8 0.7 copy.64
  (29 shorter events, 1.4 us)
Async XLA Ops:
  0.6 2.6 copy-start
  313.1 9.8 %copy-start.2 = (bf16[256,1024]{1,0:T(8,128)(2,1)S(1)}, bf16[256,1024]{1,0:T(8,128)(2,1)}, u32[]{:S(2)}) copy-start(bf16[256,1024]{1,0:T(8,128)(2,1)} %get-tuple-element.66) | copy-start | bytes 1572868
  313.1 10.6 %copy-start.1 = (bf16[256,1024]{1,0:T(8,128)(2,1)S(1)}, bf16[256,1024]{1,0:T(8,128)(2,1)}, u32[]{:S(2)}) copy-start(bf16[256,1024]{1,0:T(8,128)(2,1)} %get-tuple-element.67) | copy-start | bytes 1572868
  313.1 11.4 %copy-start.5 = (f32[8,1024]{1,0:T(8,128)S(1)}, f32[8,1024]{1,0:T(8,128)}, u32[]{:S(2)}) copy-start(f32[8,1024]{1,0:T(8,128)} %get-tuple-element.98) | copy-start | bytes 98308
  313.1 12.0 %copy-start.4 = (f32[8,1024]{1,0:T(8,128)S(1)}, f32[8,1024]{1,0:T(8,128)}, u32[]{:S(2)}) copy-start(f32[8,1024]{1,0:T(8,128)} %get-tuple-element.101) | copy-start | bytes 98308
  313.1 12.6 %copy-start.3 = (f32[40,1024]{1,0:T(8,128)S(1)}, f32[40,1024]{1,0:T(8,128)}, u32[]{:S(2)}) copy-start(f32[40,1024]{1,0:T(8,128)} %get-tuple-element.73) | copy-start | bytes 491524

commit v3 on v2

--- a/solution.py
+++ b/solution.py
@@ -16,7 +16,8 @@
 HEADS = 8
 ROWS = 256
 SEQ = 2048
-PADDED = 40
+PARTS = (16, 16, 8)
+PADDED = sum(PARTS)
 HALF = 64 * PADDED
 EPSILON = 1e-05
 THETA_BASE = 1000000.0
@@ -125,11 +126,20 @@
         self.arrived(i, stage, 3, 2, 1)
 
 
-def layouts():
-    return [
-        Layout("own", ORDERS[0], D), Layout("own", ORDERS[1], D), Layout("own", ORDERS[2], D),
-        Layout("both", ORDERS[0], HALF), Layout("both", ORDERS[1], HALF), Layout("none", ORDERS[2], D),
-    ]
+def attn_layouts():
+    return [Layout("own", ORDERS[0], D), Layout("own", ORDERS[1], D), Layout("own", ORDERS[2], D)]
+
+
+def gather_layouts():
+    shapes = attn_layouts()
+    for rows in PARTS:
+        shapes += [Layout("both", ORDERS[0], 64 * rows), Layout("both", ORDERS[1], 64 * rows), Layout("none", ORDERS[2], D)]
+    return shapes
+
+
+def scatter_layouts():
+    wide = [Layout("both", ORDERS[0], HALF), Layout("both", ORDERS[1], HALF)]
+    return attn_layouts() + wide + [Layout("none", ORDERS[2], D)] * 3
 
 
 def lanes(shape):
@@ -169,12 +179,47 @@
     return jnp.concatenate(parts, axis=0)
 
 
-def forward_kernel(x_ref, m_ref, gain_ref, qgain_ref, kgain_ref, fgain_ref, cos_ref, sin_ref, segcol_ref, segrow_ref,
-                   q_in, kv_in, o_in, g_in, u_in, d_in,
-                   wq_ref, wkv_ref, wo_ref, g_out, u_out, d_out, h_ref, qraw_ref, kraw_ref, qseq, kvseq, oseq, inv_ref, full_ref, x1_ref,
-                   h2_ref, m2_ref,
-                   wq8, wkv8, wo8, qown, kvown, orows,
-                   local_sem, core_send, core_recv, send, recv, swap_send, swap_recv, swap_local):
+def unit_sources():
+    column = lax.broadcasted_iota(jnp.int32, (1, 2 * 640), 1)
+    core, k = column // 640, column % 640
+    last = k >= 512
+    ctx = jnp.where(last, (k - 512) // 8, (k % 256) // 16)
+    row = jnp.where(last, 32 + k % 8, 16 * (k // 256) + k % 16)
+    return jnp.where(row < 36, core * 576 + ctx * 36 + row, -1)
+
+
+def spread_matrix(k, sources):
+    rows = lax.broadcasted_iota(jnp.int32, (128, 2 * 640), 0) + 128 * k
+    return jnp.where(rows == sources, 1.0, 0.0).astype(BF)
+
+
+def part_columns(y):
+    return [(0, y * 256, 256), (1, 1024 + y * 256, 256), (2, 2048 + y * 128, 128)]
+
+
+FF_BLOCK = 512
+
+
+def rope_of(table_ref):
+    table = table_ref[...]
+    low, turned = lanes(table.shape) < HDIM, pltpu.roll(table, HDIM, 1)
+    cosine, sine = jnp.where(low, table, turned), jnp.where(low, turned, table)
+    return jnp.concatenate([cosine, cosine], axis=0), jnp.concatenate([sine, sine], axis=0)
+
+
+def twice(gain_ref):
+    return jnp.concatenate([gain_ref[...], gain_ref[...]], axis=1)
+
+
+def forward_kernel(*refs):
+    (x_ref, m_ref, gain_ref, qgain_ref, kgain_ref, fgain_ref, table_ref, segs_ref, q_in, k_in, v_in,
+     o_in, gate_in, up_in, down_in) = refs[:15]
+    (wq8, wkv8, wo8, g_grad, u_grad, d_grad_a, d_grad_b, d_grad_c, h_ref, qraw_ref, kraw_ref, qseq, kvseq, oseq, inv_ref, full_ref, x1_ref,
+     out_ref, back_ref) = refs[15:34]
+    mats = refs[34:43]
+    (qown, kvown, orows, h2_ref, m2_ref, turned, g_stage, u_stage, d_stage, d_stage_c, kv_in, down_pad, *wide_shards) = refs[43:61]
+    (local_sem, core_send, core_recv, send, recv, swap_send, swap_recv, swap_local, store_sem) = refs[61:70]
+    d_grads = (d_grad_a, d_grad_b, d_grad_c)
     at = place()
     c = at["c"]
     dp, ctx = lax.axis_index("dp"), lax.axis_index("ctx")
@@ -187,98 +232,120 @@
     def _(step):
         pl.semaphore_signal(barrier, inc=1, device_id=(dp, (ctx + step) % 16), device_id_type=MESH)
 
+    sequence = pl.ds(ctx // 8, 1)
     here = (at["y"], c, at["z"], at["x"])
-    stays = [
-        pltpu.make_async_copy(q_in, wq8.at[here], local_sem.at[0]),
-        pltpu.make_async_copy(kv_in, wkv8.at[here], local_sem.at[1]),
-        pltpu.make_async_copy(o_in, wo8.at[here], local_sem.at[2]),
-        pltpu.make_async_copy(g_in.at[c], g_out.at[here], local_sem.at[3]),
-        pltpu.make_async_copy(u_in.at[c], u_out.at[here], local_sem.at[4]),
-        pltpu.make_async_copy(d_in, d_out.at[at["y"], at["z"], at["x"]], local_sem.at[5]),
-    ]
+    ring = Gather(at, [wq8, wkv8, wo8, *mats], gather_layouts(), send, recv)
+    attn, part_a, part_b, part_c = (0, 1, 2), (3, 4, 5), (6, 7, 8), (9, 10, 11)
+
+    def core_copy(slot, src, dst):
+        return pltpu.make_async_remote_copy(
+            src_ref=src, dst_ref=dst, send_sem=core_send.at[slot], recv_sem=core_recv.at[slot], device_id=partner,
+            device_id_type=MESH)
+
+    low_half = lanes((8, 128)) < HDIM
+    for k in range(4):
+        key, value = (ref[:, k * 128 : (k + 1) * 128].astype(F32) for ref in (k_in, v_in))
+        kv_in[:, k * 256 : k * 256 + 128] = jnp.where(low_half, key, pltpu.roll(value, HDIM, 1)).astype(BF)
+        kv_in[:, k * 256 + 128 : (k + 1) * 256] = jnp.where(low_half, pltpu.roll(key, HDIM, 1), value).astype(BF)
+    stays = [pltpu.make_async_copy(src, dst.at[here], local_sem.at[i]) for i, (src, dst) in enumerate(((q_in, wq8), (kv_in, wkv8), (o_in, wo8)))]
     for copy in stays:
         copy.start()
     for copy in stays:
         copy.wait()
     pl.semaphore_wait(barrier, 18)
-
-    ring = Gather(at, [wq8, wkv8, wo8, g_out, u_out, d_out], layouts(), send, recv)
-    attn, feed_mats = (0, 1, 2), (3, 4, 5)
-
-    def core_copy(slot, src, dst):
-        return pltpu.make_async_remote_copy(
-            src_ref=src, dst_ref=dst, send_sem=core_send.at[slot], recv_sem=core_recv.at[slot], device_id=partner,
-            device_id_type=MESH)
-
     for i in attn:
         ring.first(i, 0)
-    wide = [core_copy(0, g_in.at[1 - c], g_out.at[here]), core_copy(1, u_in.at[1 - c], u_out.at[here])]
-    upstream_copy = core_copy(2, m_ref, m2_ref.at[1])
-    for copy in wide:
+    upstream_copy = core_copy(6, m_ref, m2_ref.at[1])
+    upstream_copy.start()
+
+    sources = unit_sources()
+    units = jnp.concatenate(
+        [ref[:, y * 1152 : (y + 1) * 1152].astype(F32) for y in range(4) for ref in (gate_in, up_in)], axis=0).astype(BF)
+    spread = jnp.zeros((64, 2 * 640), F32)
+    for k in range(9):
+        spread = spread + dot(units[:, k * 128 : (k + 1) * 128], spread_matrix(k, sources))
+    for y in range(4):
+        for part, _, width in part_columns(y):
+            for core in range(2):
+                start = core * 640 + part * 256
+                for j in range(2):
+                    block = spread[16 * y + 8 * j : 16 * y + 8 * j + 8, start : start + width]
+                    wide_shards[2 * part + j][core, :, y * width : (y + 1) * width] = block.astype(BF)
+    down_pad[...] = jnp.concatenate([down_in[32:36, :].astype(F32), jnp.zeros((4, D), F32)], axis=0).astype(BF)
+    downs = (down_in.at[pl.ds(0, 16)], down_in.at[pl.ds(16, 16)], down_pad)
+    stays = []
+    wide = []
+    for k in range(3):
+        for j in range(2):
+            stays.append(pltpu.make_async_copy(wide_shards[2 * k + j].at[c], mats[3 * k + j].at[here], local_sem.at[3 + 3 * k + j]))
+            wide.append(core_copy(2 * k + j, wide_shards[2 * k + j].at[1 - c], mats[3 * k + j].at[here]))
+        stays.append(pltpu.make_async_copy(downs[k], mats[3 * k + 2].at[at["y"], at["z"], at["x"]], local_sem.at[5 + 3 * k]))
+    stays.append(pltpu.make_async_copy(m_ref, m2_ref.at[0], local_sem.at[12]))
+    for copy in wide + stays:
         copy.start()
-    upstream_copy.start()
     normed, _, _ = norm(x_ref[...].astype(F32), gain_ref[...])
     h_ref[...] = normed.astype(BF)
-    m2_ref[0] = m_ref[...]
+    for copy in stays:
+        copy.wait()
     for copy in wide:
         copy.wait_recv()
-    for i in feed_mats:
+    for i in part_a + part_b + part_c:
         ring.first(i, 0)
-    for i in attn:
-        ring.second(i, 0)
-    for i in attn:
-        ring.last(i, 0)
-        ring.first(i, 1)
-    for i in feed_mats:
-        ring.second(i, 0)
-    for i in attn:
-        ring.second(i, 1)
-    for i in feed_mats:
-        ring.last(i, 0)
-        ring.first(i, 1)
-    for i in attn:
-        ring.last(i, 1)
-        ring.first(i, 2)
-    for i in feed_mats:
-        ring.second(i, 1)
-    for i in attn:
-        ring.second(i, 2)
-    for i in feed_mats:
-        ring.last(i, 1)
-        ring.first(i, 2)
+
+    def second(group, stage):
+        for i in group:
+            ring.second(i, stage)
+
+    def following(group, stage):
+        for i in group:
+            ring.last(i, stage)
+            ring.first(i, stage + 1)
+
+    second(attn, 0)
+    following(attn, 0)
+    second(part_a, 0)
+    second(attn, 1)
+    following(part_a, 0)
+    following(attn, 1)
+    second(part_b + part_c, 0)
+    second(part_a, 1)
+    second(attn, 2)
+    following(part_b + part_c, 0)
     swaps = []
     eights = (wq8, wkv8, wo8)
     for i in attn:
         ring.last(i, 2)
-        copy = core_copy(3 + i, eights[i].at[:, c], eights[i].at[:, c])
+        copy = core_copy(7 + i, eights[i].at[:, c], eights[i].at[:, c])
         copy.start()
         swaps.append(copy)
 
-    def flatten(eight, flat, core):
-        @pl.loop(0, 4)
-        def _(y):
-            rows = pl.ds(pl.multiple_of(y * 256 + core * 128, 128), 128)
-            flat[rows, :] = eight[y, core].astype(F32).reshape(128, D).astype(BF)
+    following(part_a, 1)
+    second(part_b + part_c, 1)
 
     def other_rows(i):
-        core_copy(3 + i, eights[i].at[:, 1 - c], eights[i].at[:, 1 - c]).wait_recv()
-
-    flatten(wq8, wq_ref, c)
-    flatten(wkv8, wkv_ref, c)
+        core_copy(7 + i, eights[i].at[:, 1 - c], eights[i].at[:, 1 - c]).wait_recv()
+
+    def rows_of(core):
+        cols = [h_ref[:, pl.ds(pl.multiple_of((2 * y + core) * 128, 128), 128)] for y in range(4)]
+        return jnp.concatenate(cols, axis=1)
+
+    def mat_of(eight, core):
+        return eight[:, core].reshape(D // 2, D)
+
+    mine, other = rows_of(c), rows_of(1 - c)
+    query = dot(mine, mat_of(wq8, c))
     other_rows(0)
-    flatten(wq8, wq_ref, 1 - c)
-    low = h_ref[...]
-    query = dot(low, wq_ref[...])
+    query = query + dot(other, mat_of(wq8, 1 - c))
     for h in range(8):
         qraw_ref[h] = query[:, h * 128 : (h + 1) * 128]
     other_rows(1)
-    flatten(wkv8, wkv_ref, 1 - c)
-    key_value = dot(low, wkv_ref[...])
+    key_value = dot(mine, mat_of(wkv8, c)) + dot(other, mat_of(wkv8, 1 - c))
     for h in range(8):
         kraw_ref[h] = key_value[:, h * 128 : (h + 1) * 128]
 
     sums = head_sum_matrix()
-    cosine, sine = cos_ref[...], sin_ref[...]
+    cosine, sine = rope_of(table_ref)
+    qgain, kgain = twice(qgain_ref), twice(kgain_ref)
 
     def rotated(raw, gain):
         factor = lax.rsqrt(split_dot(raw * raw, sums) * (1.0 / HDIM) + EPSILON)
@@ -294,9 +361,9 @@
     def _(step):
         h = (ctx + step) % 8
         raw = qraw_ref[h]
-        qown[h] = rotated(raw, qgain_ref[...]).astype(BF)
+        qown[h] = rotated(raw, qgain).astype(BF)
         raw = kraw_ref[h]
-        kvown[h] = jnp.where(lanes(raw.shape) < HDIM, rotated(raw, kgain_ref[...]), raw).astype(BF)
+        kvown[h] = jnp.where(lanes(raw.shape) < HDIM, rotated(raw, kgain), raw).astype(BF)
         for s in range(2):
             to = s * 8 + h
             rows = pl.ds(s * 128, 128)
@@ -312,9 +379,6 @@
                 pltpu.make_async_copy(qown.at[h, rows], qseq.at[ctx], swap_local.at[1]).start()
 
     other_rows(2)
-    flatten(wo8, wo_ref, c)
-    flatten(wo8, wo_ref, 1 - c)
-
     low_lane = lanes((BLOCK, 128)) < HDIM
 
     def arrive(source):
@@ -336,13 +400,13 @@
         second = pltpu.roll(q.astype(F32), HDIM, 1).astype(BF)
         stacked = jnp.concatenate([jnp.where(low_lane, q, zero), jnp.where(low_lane, second, zero)], axis=0)
         rows = pl.ds(pl.multiple_of(block * BLOCK, BLOCK), BLOCK)
-        seg_q = segcol_ref[rows, :]
+        seg_q = segment_column(segs_ref[sequence, rows])
         seg_q = jnp.concatenate([seg_q, seg_q], axis=0)
 
         def part(j, total, diagonal):
             kv = kvseq[pl.ds(2 * j, 2)].reshape(BLOCK, 128)
             scores = dot_cols(stacked, kv)
-            allowed = seg_q == segrow_ref[:, pl.ds(pl.multiple_of(j * BLOCK, BLOCK), BLOCK)]
+            allowed = seg_q == segs_ref[sequence, pl.ds(pl.multiple_of(j * BLOCK, BLOCK), BLOCK)]
             if diagonal:
                 query = lax.broadcasted_iota(jnp.int32, (2 * BLOCK, BLOCK), 0) % BLOCK
                 allowed = allowed & (query >= lanes((2 * BLOCK, BLOCK)))
@@ -368,14 +432,17 @@
             def _():
                 pltpu.make_async_copy(oseq.at[to], orows.at[ctx], swap_local.at[2]).start()
 
-    @pl.loop(0, 6)
+    queries(0)
+    second(part_a, 2)
+    following(part_b + part_c, 1)
+
+    @pl.loop(1, 7)
     def _(block):
         queries(block)
 
-    for i in feed_mats:
-        ring.second(i, 2)
-
-    @pl.loop(6, 8)
+    second(part_b + part_c, 2)
+
+    @pl.loop(7, 8)
     def _(block):
         queries(block)
 
@@ -391,14 +458,87 @@
 
     attended = heads_to_rows(orows)
     full_ref[...] = attended
-    residual = x_ref[...].astype(F32) + dot(attended, wo_ref[...])
+    residual = x_ref[...].astype(F32) + dot(attended, wo8[...].reshape(D, D))
     x1_ref[...] = residual
     normed, _, _ = norm(residual, fgain_ref[...])
     h2_ref[0] = normed.astype(BF)
-    mid_copy = core_copy(6, h2_ref.at[0], h2_ref.at[1])
+    mid_copy = core_copy(10, h2_ref.at[0], h2_ref.at[1])
     mid_copy.start()
-    for i in feed_mats:
-        ring.last(i, 2)
+    out_ref[...] = jnp.zeros_like(out_ref)
+    back_ref[...] = jnp.zeros_like(back_ref)
+    upstream_copy.wait()
+    mid_copy.wait()
+    turned[...] = jnp.transpose(h2_ref[...].reshape(2 * ROWS, D))
+
+    def store_copies(part, step, slot):
+        cols = pl.ds(pl.multiple_of(step * FF_BLOCK, FF_BLOCK), FF_BLOCK)
+        where = (slice(None),) * 5 + (cols,)
+        if part < 2:
+            down, rows = d_stage, d_grads[part].at[pl.ds(2 * slot, 2)]
+        else:
+            down, rows = d_stage_c, d_grads[2]
+        return [
+            pltpu.make_async_copy(g_stage, g_grad.at[where], store_sem.at[0]),
+            pltpu.make_async_copy(u_stage, u_grad.at[where], store_sem.at[1]),
+            pltpu.make_async_copy(down, rows, store_sem.at[2 + (part == 2)]),
+        ]
+
+    def feed(part, slot):
+        rows = PARTS[part]
+        gate_mat, up_mat, down_mat = (mats[3 * part + j] for j in range(3))
+        step = 2 * part + slot
+        cols = pl.ds(pl.multiple_of(slot * FF_BLOCK, FF_BLOCK), FF_BLOCK)
+        wg = gate_mat.reshape(D, 64 * rows)[:, cols]
+        wu = up_mat.reshape(D, 64 * rows)[:, cols]
+        wd = down_mat.reshape(64 * rows, D)[cols, :]
+        low, upstream = h2_ref[...].reshape(2 * ROWS, D), m2_ref[...].reshape(2 * ROWS, D)
+        gate = dot(low, wg)
+        up = dot(low, wu)
+        sig = jax.nn.sigmoid(gate)
+        silu = gate * sig
+        hidden = (silu * up).astype(BF)
+        slope = dot_cols(upstream, wd)
+        gate_grad = (slope * up * sig * (1.0 + gate * (1.0 - sig))).astype(BF)
+        up_grad = (slope * silu).astype(BF)
+
+        def freed():
+            g_copy, u_copy, d_copy = store_copies(min(part, 1), step, 0)
+            g_copy.wait()
+            u_copy.wait()
+            if part < 2:
+                d_copy.wait()
+
+        if part == 0:
+            pl.when(slot > 0)(freed)
+        else:
+            freed()
+        for y in range(0, 4, 2):
+            left = turned[y * 256 : (y + 2) * 256, :]
+            g_stage[y : y + 2] = dot(left, gate_grad).astype(BF).reshape(2, 2, 4, 4, 8, FF_BLOCK)
+            u_stage[y : y + 2] = dot(left, up_grad).astype(BF).reshape(2, 2, 4, 4, 8, FF_BLOCK)
+        down_grad = dot_rows(hidden, upstream).astype(BF)
+        if part < 2:
+            d_stage[...] = down_grad.reshape(2, 4, 4, 16, D)
+        else:
+            d_stage_c[...] = down_grad.reshape(4, 4, 4, 8, D)
+        for copy in store_copies(part, step, slot):
+            copy.start()
+        out_ref[...] += dot(hidden, wd)
+        back_ref[...] += dot_cols(gate_grad, wg)
+        back_ref[...] += dot_cols(up_grad, wu)
+
+    for part, group in enumerate((part_a, part_b, part_c)):
+        for i in group:
+            ring.last(i, 2)
+        if part < 2:
+            @pl.loop(0, 2)
+            def _(slot):
+                feed(part, slot)
+        else:
+            feed(part, 0)
+
+    for copy in store_copies(1, 3, 1)[2:] + store_copies(2, 4, 0):
+        copy.wait()
 
     @pl.loop(0, 16)
     def _(to):
@@ -408,84 +548,36 @@
             swap_copy(1, qown.at[0, pl.ds(0, 128)], qseq.at[to], to, to).wait_send()
             swap_copy(2, oseq.at[to], orows.at[to], to, to).wait_send()
 
-    for copy in wide + swaps:
-        copy.wait_send()
-    upstream_copy.wait()
-    mid_copy.wait()
-    for copy in ring.started:
+    for copy in wide + swaps + ring.started:
         copy.wait_send()
 
 
 def forward(*arrays):
     shape = jax.ShapeDtypeStruct
     dma = pltpu.SemaphoreType.DMA
+    attn = shape((4, 2, 4, 4, 8, D), BF)
     wide = shape((4, 2, 4, 4, 8, HALF), BF)
+    rows, heads = shape((ROWS, D), F32), shape((16, 128, 128), BF)
+    mats = []
+    for part in PARTS:
+        mats += [pltpu.VMEM((4, 2, 4, 4, 8, 64 * part), BF)] * 2 + [pltpu.VMEM((4, 4, 4, part, D), BF)]
+    raw = shape((8, ROWS, 128), F32)
+    both = shape((2 * ROWS, D), F32)
     return pl.pallas_call(
         forward_kernel,
         out_shape=(
-            shape((D, D), BF), shape((D, D), BF), shape((D, D), BF), wide, wide, shape((4, 4, 4, PADDED, D), BF),
-            shape((ROWS, D), BF), shape((8, ROWS, 128), F32), shape((8, ROWS, 128), F32), shape((16, 128, 128), BF),
-            shape((16, 128, 128), BF), shape((16, 128, 128), BF), shape((2, SEQ), F32), shape((ROWS, D), BF), shape((ROWS, D), F32),
-            shape((2, ROWS, D), BF), shape((2, ROWS, D), BF),
+            attn, attn, attn, wide, wide, *(shape((4, 4, 4, part, D), BF) for part in PARTS),
+            shape((ROWS, D), BF), raw, raw, heads, heads, heads, shape((2, SEQ), F32), shape((ROWS, D), BF), rows, both, both,
         ),
-        in_specs=[vmem()] * 13 + [hbm()] * 3,
-        out_specs=[vmem()] * 3 + [hbm()] * 3 + [vmem()] * 11,
-        scratch_shapes=[pltpu.VMEM((4, 2, 4, 4, 8, D), BF)] * 3 + [pltpu.VMEM((8, ROWS, 128), BF)] * 2 + [pltpu.VMEM((16, 128, 128), BF)]
-        + [dma((6,)), dma((7,)), dma((7,)), dma((6, 3, 4)), dma((6, 3, 4)), dma((3, 16)), dma((3, 16)), dma((3,))],
+        in_specs=[vmem()] + [hbm()] + [vmem()] * 13,
+        out_specs=[vmem()] * 3 + [hbm()] * 5 + [vmem()] * 11,
+        scratch_shapes=mats + [pltpu.VMEM((8, ROWS, 128), BF)] * 2 + [pltpu.VMEM((16, 128, 128), BF)] + [pltpu.VMEM((2, ROWS, D), BF)] * 2
+        + [pltpu.VMEM((D, 2 * ROWS), BF)] + [pltpu.VMEM((4, 2, 4, 4, 8, FF_BLOCK), BF)] * 2
+        + [pltpu.VMEM((2, 4, 4, 16, D), BF), pltpu.VMEM((4, 4, 4, 8, D), BF)]
+        + [pltpu.VMEM((8, D), BF)] * 2 + [pltpu.VMEM((2, 8, 64 * part), BF) for part in PARTS for _ in range(2)]
+        + [dma((13,)), dma((11,)), dma((11,)), dma((12, 3, 4)), dma((12, 3, 4)), dma((3, 16)), dma((3, 16)), dma((3,)), dma((4,))],
         compiler_params=params(collective_id=0, has_side_effects=True),
     )(*arrays)
-
-
-FF_BLOCK = 512
-
-
-def feed_kernel(h_ref, m_ref, wg_ref, wu_ref, wd_ref, out_ref, back_ref, gg_ref, gu_ref, gd_ref, turned):
-    step = pl.program_id(0)
-
-    @pl.when(step == 0)
-    def _():
-        out_ref[...] = jnp.zeros_like(out_ref)
-        back_ref[...] = jnp.zeros_like(back_ref)
-        turned[...] = jnp.transpose(h_ref[...])
-
-    low, upstream = h_ref[...], m_ref[...]
-    gate = dot(low, wg_ref[...])
-    up = dot(low, wu_ref[...])
-    sig = jax.nn.sigmoid(gate)
-    silu = gate * sig
-    hidden = (silu * up).astype(BF)
-    out_ref[...] += dot(hidden, wd_ref[...])
-    slope = dot_cols(upstream, wd_ref[...])
-    gate_grad = (slope * up * sig * (1.0 + gate * (1.0 - sig))).astype(BF)
-    up_grad = (slope * silu).astype(BF)
-    back_ref[...] += dot_cols(gate_grad, wg_ref[...]) + dot_cols(up_grad, wu_ref[...])
-    gd_ref[...] = dot_rows(hidden, upstream).astype(BF)
-    gg_ref[...] = dot(turned[...], gate_grad).astype(BF)
-    gu_ref[...] = dot(turned[...], up_grad).astype(BF)
-
-
-def feed(h, m, wg, wu, wd):
-    full = lambda shape: pl.BlockSpec(shape, lambda i: (0,) * len(shape))
-    wide = pl.BlockSpec((D, FF_BLOCK), lambda i: (0, i))
-    tall = pl.BlockSpec((FF_BLOCK, D), lambda i: (i, 0))
-    both = 2 * ROWS
-    return pl.pallas_call(
-        feed_kernel,
-        grid=(HALF // FF_BLOCK,),
-        out_shape=(
-            jax.ShapeDtypeStruct((both, D), F32), jax.ShapeDtypeStruct((both, D), F32),
-            jax.ShapeDtypeStruct((D, HALF), BF), jax.ShapeDtypeStruct((D, HALF), BF), jax.ShapeDtypeStruct((HALF, D), BF),
-        ),
-        in_specs=[full((both, D)), full((both, D)), wide, wide, tall],
-        out_specs=[full((both, D)), full((both, D)), wide, wide, tall],
-        scratch_shapes=[pltpu.VMEM((D, both), BF)],
-        compiler_params=params(),
-    )(h, m, wg, wu, wd)
-
-
-def norm_back(upstream, gain, unit, factor):
-    scaled = upstream * gain
-    return factor * (scaled - unit * jnp.mean(scaled * unit, axis=-1, keepdims=True))
 
 
 class Scatter:
@@ -625,16 +717,21 @@
 GAIN_ROWS = 24
 
 
+def segment_column(row):
+    return jnp.transpose(jnp.broadcast_to(row.astype(F32), (128, row.shape[1])))[:, :1].astype(jnp.int32)
+
+
 def backward_kernel(*refs):
-    (x_ref, m_ref, gain_ref, qgain_ref, kgain_ref, fgain_ref, cos_ref, sin_ref, segcol_ref, segrow_ref, x1_ref, out_hbm, back_hbm,
-     full_ref, qseq, kvseq, oseq, inv_ref, h_ref, qraw_ref, kraw_ref, wo_hbm, wq_hbm, wkv_hbm, g_hbm, u_hbm, d_hbm) = refs[:27]
-    (y_ref, yin_ref, q_fin, kv_fin, o_fin, g_fin, u_fin, d_fin, gains_out) = refs[27:36]
+    (x_ref, m_ref, gain_ref, qgain_ref, kgain_ref, fgain_ref, table_ref, segs_ref, x1_ref, out_hbm, back_hbm,
+     full_ref, qseq, kvseq, oseq, inv_ref, h_ref, qraw_ref, kraw_ref, wo_hbm, wq_hbm, wkv_hbm, g_hbm, u_hbm, *d_hbm) = refs[:27]
+    (y_ref, yin_ref, q_fin, k_out, v_out, o_fin, g_out, u_out, d_out, attn_gain_out, ffn_gain_out, q_gain_out, k_gain_out) = refs[27:40]
     (gq, gkv, go, out_own, back_own, out_other, back_other, do_own, do_seq, dq_own, dkv_own, dq_in, dkv_in, acc, dq_full, dkv_full,
-     gains, gain_slots, wide_g, wide_u, first_mat, second_mat) = refs[36:58]
-    cores = refs[58:61]
-    own = [None, None, None, *refs[61:64]]
-    bufs = [refs[64 + 6 * i : 70 + 6 * i] for i in range(6)]
-    (core_send, core_recv, local_sem, send, recv, load_sem, swap_send, swap_recv, swap_local, gain_send, gain_recv) = refs[100:111]
+     gains, gain_slots, wide_g, wide_u, first_mat, second_mat) = refs[40:62]
+    cores = refs[62:65]
+    own = [None, None, None, *refs[65:70]]
+    bufs = [refs[70 + 6 * i : 76 + 6 * i] for i in range(8)]
+    (core_send, core_recv, local_sem, send, recv, load_sem, swap_send, swap_recv, swap_local, gain_send, gain_recv) = refs[118:129]
+    kv_fin, g_fin, u_fin, *d_fins, segcol_ref = refs[129:136]
     at = place()
     c = at["c"]
     dp, ctx = lax.axis_index("dp"), lax.axis_index("ctx")
@@ -665,9 +762,9 @@
     swaps = [core_copy(0, back_hbm.at[rows_other], back_other), core_copy(1, out_hbm.at[rows_other], out_other)]
     for copy in swaps:
         copy.start()
-    fins = [q_fin, kv_fin, o_fin, wide_g, wide_u, d_fin]
-    ring = Scatter(at, [gq, gkv, go, g_hbm, u_hbm, d_hbm], layouts(), bufs, own, fins, send, recv, load_sem)
-    attn, feed_mats = (0, 1, 2), (3, 4, 5)
+    fins = [q_fin, kv_fin, o_fin, wide_g, wide_u, *d_fins]
+    ring = Scatter(at, [gq, gkv, go, g_hbm, u_hbm, *d_hbm], scatter_layouts(), bufs, own, fins, send, recv, load_sem)
+    attn, feed_mats = (0, 1, 2), (3, 4, 5, 6, 7)
     for i in feed_mats:
         ring.first(i, 0)
 
@@ -682,7 +779,7 @@
         gains[8 + k : 9 + k, :] = jnp.sum(upstream[:, k * 128 : (k + 1) * 128] * unit[:, k * 128 : (k + 1) * 128], axis=0, keepdims=True)
     dx1 = m_ref[...].astype(F32) + norm_back(upstream, gain, unit, factor)
     back_own[...] = dx1
-    do = dot_cols(dx1.astype(BF), first_mat[...]).astype(BF)
+    do = dot_cols(dx1.astype(BF), first_mat[...].reshape(D, D)).astype(BF)
     for s in range(2):
         for h in range(8):
             do_own[s * 8 + h] = do[s * 128 : (s + 1) * 128, h * 128 : (h + 1) * 128]
@@ -717,6 +814,10 @@
         swap_start(0, do_own, do_seq, (ctx + step) % 16)
 
     acc[...] = jnp.zeros_like(acc)
+    sequence = pl.ds(ctx // 8, 1)
+    for k in range(SEQ // BLOCK):
+        rows = slice(k * BLOCK, (k + 1) * BLOCK)
+        segcol_ref[rows, :] = segment_column(segs_ref[sequence, rows])
     swaps[1].wait()
     y_ref[...] = (residual + out_own[...] + out_other[...]).astype(BF)
 
@@ -750,7 +851,8 @@
         sums = dot_cols(pick, high) + dot_cols(pick, rest)
         row_dots = jnp.concatenate([sums[0:1], sums[1:2]], axis=1)
         inv = jnp.concatenate([inv_ref[0:1, rows], inv_ref[1:2, rows]], axis=1)
-        seg_q = jnp.concatenate([segrow_ref[:, rows], segrow_ref[:, rows]], axis=1)
+        seg_q = segs_ref[sequence, rows]
+        seg_q = jnp.concatenate([seg_q, seg_q], axis=1)
 
         def part(j, total, diagonal):
             kv = kvseq[pl.ds(2 * j, 2)].reshape(BLOCK, 128)
@@ -785,7 +887,8 @@
     def _(step):
         queries(7 - step)
 
-    cosine, sine = cos_ref[...], sin_ref[...]
+    cosine, sine = rope_of(table_ref)
+    qgain, kgain = twice(qgain_ref), twice(kgain_ref)
     head_sums = head_sum_matrix()
     wide_lane = lanes((ROWS, 128)) < HDIM
 
@@ -807,11 +910,11 @@
     for h in range(8):
         cols = slice(h * 128, (h + 1) * 128)
         upstream = jnp.concatenate([dq_in[h], dq_in[8 + h]], axis=0).astype(F32)
-        pre, terms = head_back(qraw_ref[h], upstream, qgain_ref[...])
+        pre, terms = head_back(qraw_ref[h], upstream, qgain)
         qterms = qterms + terms
         dq_full[:, cols] = pre.astype(BF)
         upstream = jnp.concatenate([dkv_in[h], dkv_in[8 + h]], axis=0).astype(F32)
-        pre, terms = head_back(kraw_ref[h], upstream, kgain_ref[...])
+        pre, terms = head_back(kraw_ref[h], upstream, kgain)
         kterms = kterms + terms
         dkv_full[:, cols] = jnp.where(wide_lane, pre, upstream).astype(BF)
     gains[16:17, :] = qterms
@@ -833,7 +936,7 @@
         ring.first(i, 0)
 
     query_mat.wait()
-    dh = dot_cols(dq_full[...], first_mat[...]) + dot_cols(dkv_full[...], second_mat[...])
+    dh = dot_cols(dq_full[...], first_mat[...].reshape(D, D)) + dot_cols(dkv_full[...], second_mat[...].reshape(D, D))
     gain = gain_ref[...]
     _, unit, factor = norm(x_ref[...].astype(F32), gain)
     for k in range(8):
@@ -912,8 +1015,35 @@
     finals[-1].start()
     for slot, fin in ((5, g_fin), (6, u_fin)):
         core_copy(slot, fin.at[1 - c], fin.at[1 - c]).wait_recv()
+    columns = []
+    for y in range(4):
+        for fin in (g_fin, u_fin):
+            columns.append(jnp.concatenate([fin[core, :, start : start + width] for core in range(2) for _, start, width in part_columns(y)], axis=1))
+    columns = jnp.concatenate(columns, axis=0)
+    high = columns.astype(BF)
+    rest = (columns - high.astype(F32)).astype(BF)
+    sources = unit_sources()
+    for k in range(9):
+        matrix = spread_matrix(k, sources)
+        units = dot_cols(high, matrix) + dot_cols(rest, matrix)
+        for y in range(4):
+            where = slice(y * 1152 + k * 128, y * 1152 + (k + 1) * 128)
+            g_out[:, where] = units[16 * y : 16 * y + 8]
+            u_out[:, where] = units[16 * y + 8 : 16 * y + 16]
     core_copy(7, gain_slots.at[3, 1 - c], gain_slots.at[3, 1 - c]).wait_recv()
-    gains_out[...] = gain_slots[3, 0] + gain_slots[3, 1]
+    total = gain_slots[3, 0] + gain_slots[3, 1]
+    attn_gain_out[...] = total[:8]
+    ffn_gain_out[...] = total[8:16]
+    q_gain_out[...] = (total[16:17] + pltpu.roll(total, HDIM, 1)[16:17])[:, :HDIM]
+    k_gain_out[...] = total[17:18, :HDIM]
+    low_half = lanes((8, 128)) < HDIM
+    for k in range(4):
+        even, odd = kv_fin[:, k * 256 : k * 256 + 128], kv_fin[:, k * 256 + 128 : (k + 1) * 256]
+        k_out[:, k * 128 : (k + 1) * 128] = jnp.where(low_half, even, pltpu.roll(odd, HDIM, 1))
+        v_out[:, k * 128 : (k + 1) * 128] = jnp.where(low_half, pltpu.roll(even, HDIM, 1), odd)
+    d_out[0:16, :] = d_fins[0][...]
+    d_out[16:32, :] = d_fins[1][...]
+    d_out[32:36, :] = d_fins[2][0:4, :]
 
     @pl.loop(0, 16)
     def _(to):
@@ -931,83 +1061,73 @@
     shape = jax.ShapeDtypeStruct
     dma = pltpu.SemaphoreType.DMA
     small = shape((8, D), F32)
-    wide = shape((2, 8, HALF), F32)
     block = pltpu.VMEM((16, 128, 128), BF)
     own = pltpu.VMEM((ROWS, D), F32)
     scratch = [pltpu.VMEM((4, 2, 4, 4, 8, D), BF)] * 3 + [own] * 4 + [block] * 6
     scratch += [pltpu.VMEM((SEQ // BLOCK, BLOCK, 128), F32)] + [pltpu.VMEM((ROWS, D), BF)] * 2
     scratch += [pltpu.VMEM((GAIN_ROWS, 128), F32), pltpu.VMEM((4, 4, GAIN_ROWS, 128), F32)] + [pltpu.VMEM((2, 8, HALF), F32)] * 2
-    scratch += [pltpu.VMEM((D, D), BF)] * 2 + [pltpu.VMEM((4, 4, 4, 8, D), BF)] * 3
-    lays = layouts()
-    shapes = [stage_shapes(lay, PADDED if lay.kind == "none" else 8) for lay in lays]
-    scratch += [pltpu.VMEM(shapes[i][0], BF) for i in (3, 4, 5)]
+    scratch += [pltpu.VMEM((4, 2, 4, 4, 8, D), BF)] * 2 + [pltpu.VMEM((4, 4, 4, 8, D), BF)] * 3
+    shapes = [stage_shapes(lay, rows) for lay, rows in zip(scatter_layouts(), (8,) * 5 + PARTS)]
+    scratch += [pltpu.VMEM(shapes[i][0], BF) for i in range(3, 8)]
     for group in shapes:
         scratch += [pltpu.VMEM(s, BF) for s in group]
     scratch += [
-        dma((8,)), dma((8,)), dma((5,)), dma((6, 3, 6)), dma((6, 3, 6)), dma((6, 2)), dma((3, 16)), dma((3, 16)), dma((3,)), dma((3, 3)),
+        dma((8,)), dma((8,)), dma((5,)), dma((8, 3, 6)), dma((8, 3, 6)), dma((8, 2)), dma((3, 16)), dma((3, 16)), dma((3,)), dma((3, 3)),
         dma((3, 3)),
     ]
+    scratch += [pltpu.VMEM((8, D), F32)] + [pltpu.VMEM((2, 8, HALF), F32)] * 2 + [pltpu.VMEM((part, D), F32) for part in PARTS]
+    scratch += [pltpu.VMEM((SEQ, 1), jnp.int32)]
     return pl.pallas_call(
         backward_kernel,
         out_shape=(
-            shape((ROWS, D), BF), shape((ROWS, D), BF), small, small, small, wide, wide, shape((PADDED, D), F32),
-            shape((GAIN_ROWS, 128), F32),
+            shape((ROWS, D), BF), shape((ROWS, D), BF), small, shape((8, D // 2), F32), shape((8, D // 2), F32), small, shape((8, 4608), F32),
+            shape((8, 4608), F32), shape((36, D), F32), shape((8, 128), F32), shape((8, 128), F32), shape((1, HDIM), F32),
+            shape((1, HDIM), F32),
         ),
-        in_specs=[vmem()] * 11 + [hbm()] * 2 + [vmem()] * 8 + [hbm()] * 6,
-        out_specs=[vmem()] * 9,
+        in_specs=[vmem()] * 9 + [hbm()] * 2 + [vmem()] * 8 + [hbm()] * 8,
+        out_specs=[vmem()] * 13,
         scratch_shapes=scratch,
         compiler_params=params(collective_id=1, has_side_effects=True),
     )(*arrays)
 
 
-def tables(first_row):
-    places = first_row + jnp.arange(128, dtype=jnp.int32)
-    frequency = THETA_BASE ** (-jnp.arange(0, HDIM, 2, dtype=F32) / HDIM)
-    angles = places.astype(F32)[:, None] * frequency[None, :]
-    cosine, sine = jnp.tile(jnp.cos(angles), (2, 4)), jnp.tile(jnp.sin(angles), (2, 4))
-    return cosine, sine
-
-
-def pair_heads(wk, wv):
-    rows = wk.shape[0]
-    return jnp.concatenate([wk.reshape(rows, 8, 1, HDIM), wv.reshape(rows, 8, 1, HDIM)], axis=2).reshape(rows, D)
-
-
-def by_core(w):
-    w = w.reshape(8, 4, 2, 16, 36)
-    w = jnp.pad(w, ((0, 0), (0, 0), (0, 0), (0, 0), (0, PADDED - 36)))
-    return w.transpose(2, 0, 1, 3, 4).reshape(2, 8, HALF)
-
-
-def from_core(w):
-    w = w.reshape(2, 8, 4, 16, PADDED)[..., :36]
-    return w.transpose(1, 2, 0, 3, 4).reshape(8, 4608)
+def results_kernel(*refs):
+    count = len(refs) // 2
+    for source, target in zip(refs[:count], refs[count:]):
+        target[...] = source[...]
+
+
+def results(arrays):
+    return pl.pallas_call(
+        results_kernel,
+        out_shape=tuple(jax.ShapeDtypeStruct(a.shape, a.dtype) for a in arrays),
+        in_specs=[vmem()] * len(arrays),
+        out_specs=[vmem()] * len(arrays),
+        compiler_params=params(),
+    )(*arrays)
+
+
+def rope_table(first_row):
+    places = first_row + lax.broadcasted_iota(jnp.int32, (128, 128), 0)
+    lane = lax.broadcasted_iota(jnp.int32, (128, 128), 1)
+    frequency = THETA_BASE ** (-2.0 * (lane % (HDIM // 2)).astype(F32) / HDIM)
+    angles = places.astype(F32) * frequency
+    return jnp.where(lane < HDIM, jnp.cos(angles), jnp.sin(angles))
 
 
 def local(block_in, segment_ids, attn_gain, w_query, w_key, w_value, query_gain, key_gain, w_out, ffn_gain, w_gate, w_up, w_down, out_grad):
-    ctx = lax.axis_index("ctx")
     x = block_in.reshape(ROWS, D)
     m = out_grad.reshape(ROWS, D)
-    cosine, sine = tables(ctx * 128)
     row = lambda v: v.reshape(1, -1)
-    qgain, kgain = row(jnp.tile(query_gain, 2)), row(jnp.tile(key_gain, 2))
-    seg = lax.dynamic_index_in_dim(segment_ids, ctx // 8, 0, keepdims=False)
-    segcol, segrow = seg.reshape(SEQ, 1), seg.reshape(1, SEQ)
-
-    (wq, wkv, wo, wg, wu, wd, h1, qraw, kraw, q, kv, o, inv, attended, x1, h2, m2) = forward(
-        x, m, row(attn_gain), qgain, kgain, row(ffn_gain), cosine, sine, segcol, segrow,
-        w_query, pair_heads(w_key, w_value), w_out, by_core(w_gate), by_core(w_up), jnp.pad(w_down, ((0, PADDED - 36), (0, 0))))
-    wg, wu, wd = wg.reshape(D, HALF), wu.reshape(D, HALF), wd.reshape(HALF, D)
-    out, back, gg, gu, gd = feed(h2.reshape(2 * ROWS, D), m2.reshape(2 * ROWS, D), wg, wu, wd)
-    y, y_in, gq, gkv, gout, gg, gu, gd, terms = backward(
-        x, m, row(attn_gain), qgain, kgain, row(ffn_gain), cosine, sine, segcol, segrow, x1, out, back, attended, q, kv, o, inv, h1,
-        qraw, kraw, wo, wq, wkv, gg.reshape(4, 2, 4, 4, 8, HALF), gu.reshape(4, 2, 4, 4, 8, HALF), gd.reshape(4, 4, 4, PADDED, D))
-    terms = terms.reshape(-1)
-    gkv = gkv.reshape(8, 8, 2, HDIM)
+    gains = row(attn_gain), row(query_gain), row(key_gain), row(ffn_gain)
+    table = rope_table(lax.axis_index("ctx") * 128)
+    (wq, wkv, wo, gg, gu, gda, gdb, gdc, h1, qraw, kraw, q, kv, o, inv, attended, x1, out, back) = forward(
+        x, m, *gains, table, segment_ids, w_query, w_key, w_value, w_out, w_gate, w_up, w_down)
+    y, y_in, gq, gk, gv, gout, gg, gu, gd, attn_terms, ffn_terms, q_terms, k_terms = results(backward(
+        x, m, *gains, table, segment_ids, x1, out, back, attended, q, kv, o, inv, h1, qraw, kraw, wo, wq, wkv, gg, gu, gda, gdb, gdc))
     return (
-        y.reshape(2, 128, D), y_in.reshape(2, 128, D), gq, gkv[:, :, 0].reshape(8, 512), gkv[:, :, 1].reshape(8, 512), gout,
-        from_core(gg), from_core(gu), gd[:36], terms[:D], terms[2 * D : 2 * D + 64] + terms[2 * D + 64 : 2 * D + 128],
-        terms[2 * D + 128 : 2 * D + 192], terms[D : 2 * D],
+        y.reshape(2, 128, D), y_in.reshape(2, 128, D), gq, gk, gv, gout, gg, gu, gd, attn_terms.reshape(D), q_terms.reshape(HDIM),
+        k_terms.reshape(HDIM), ffn_terms.reshape(D),
     )
 
 

time: 328 us -> 295 us (0.90)
  local copies, waits for them, and re-layouts: 26.8 us -> 0 us
  Pallas kernels: 297 us -> 292 us
    reshape x14 -> x0, local copies, waits for them, and re-layouts: 14 us -> none  [the longest x2 3.06 us: by_core(): w = w.reshape(8, 4, 2, 16, 36)]
    pallas_call x2, Pallas kernels: 151 us -> 139 us  [the longest x1 136 us: forward(): pl.pallas_call(forward_kernel, out_shape=(attn, attn, attn, wide, wide, *...]
    pallas_call x1, Pallas kernels: 146 us -> 153 us  [backward(): pl.pallas_call(backward_kernel, out_shape=(shape((ROWS, D), BF), shape((R...]
    another operation x10 -> x0, local copies, waits for them, and re-layouts: 5.43 us -> none  [the longest x2 1.31 us: local(): qgain, kgain = (row(jnp.tile(query_gain, 2)), row(jnp.tile(key_gain, 2)))]
    unnamed x19 -> x0, local copies, waits for them, and re-layouts: 3.53 us -> none
where the time goes in v3:
time: 295 us; the launch traced here: 294 us
  Pallas kernels  292 us (99%)
    pallas_call x1, Pallas kernels, backward(): pl.pallas_call(backward_kernel, out_shape=(shape((ROWS, D), BF), shape((R...  153 us
    pallas_call x1, Pallas kernels, forward(): pl.pallas_call(forward_kernel, out_shape=(attn, attn, attn, wide, wide, *...  136 us

profile of v3, /device:TPU:0, one launch (start us, length us, event | category | flops | bytes accessed | tf_op | source)
XLA Modules:
  0.0 294.3 jit_solution(4938929971776102080)
XLA Ops:
  0.7 0.9 sine_select_fusion.refs_6_
  1.6 136.4 %shard_map.237 = (bf16[4,2,4,4,8,1024]{5,4,3,2,1,0:T(8,128)(2,1)}, bf16[4,2,4,4,8,1024]{5,4,3,2,1,0:T(8,128)(2,1)}, bf16[4,2,4,4,8,1024]{5,4,3,2,1,0:T(8,128)(2,...) custom-call(bf16[256,1024]{1,0:T(8,128)(2,1)} %bitcast.12, ...), custom_call_target="tpu_custom_call" | custom-call | tf_op jit(solution)/shard_map/pallas_call | solution.py:566
  138.1 153.4 %shard_map.238 = (bf16[256,1024]{1,0:T(8,128)(2,1)}, bf16[256,1024]{1,0:T(8,128)(2,1)}, f32[8,1024]{1,0:T(8,128)}, f32[8,512]{1,0:T(8,128)}, f32[8,512]{1,0:T(8,...) custom-call(bf16[256,1024]{1,0:T(8,128)(2,1)} %bitcast.13, ...), custom_call_target="tpu_custom_call" | custom-call | tf_op jit(solution)/shard_map/pallas_call | solution.py:1080
  291.5 2.6 shard_map.239
  (3 shorter events, 0.0 us)
